TPU v7x, 32 devices: a whole 2x2x4 slice. The times are simulated.
32 devices in a mesh: row: 8 (over y, x, core), col: 4 (over z).
Axes of the slice: x: 2, y: 2, z: 4, core: 2. Of those that a mesh axis runs over, the one named last changes fastest.
Arguments:
- latents: bfloat16 [512, 6144], P('col', 'row'), may hold values from -6 to 6
- w_in: bfloat16 [6144, 24576], P('row', 'col'), may hold values from -0.078125 to 0.078125
- w_out: bfloat16 [24576, 6144], P('col', 'row'), may hold values from -0.0390625 to 0.0390625
- cotangent: bfloat16 [512, 6144], P('col', 'row'), may hold values from -0.625 to 0.625
Outputs:
- mixed: bfloat16 [512, 6144], P('col', 'row')
- grad_w_in: bfloat16 [6144, 24576], P('row', 'col')
- grad_w_out: bfloat16 [24576, 6144], P('col', 'row')
All inputs are finite; a program needn't handle non-finite values.
Results may differ from a plain program's by a relative error of at most 0.03.
Values may be sent and summed in bfloat16 or wider, within the bound.
No kernel may reach another device: no remote copies, remote signals or barrier semaphores. Data moves between devices by JAX's collectives and lax.ppermute only.
A program may use at most 128 MiB of HBM per device.

v0:
```python
import jax
import jax.numpy as jnp
from jax import lax
from jax.sharding import PartitionSpec as P

f32 = jnp.float32
bf16 = jnp.bfloat16


def gelu_parts(hidden):
    cdf = 0.5 * (1.0 + jax.scipy.special.erf(hidden * 0.7071067811865476))
    pdf = jnp.exp(-0.5 * hidden * hidden) * 0.3989422804014327
    return (hidden * cdf, cdf + hidden * pdf)


def add_and_split(v, got):
    rows = v.shape[0]
    total = (v.astype(f32) + got.astype(f32)).astype(bf16)
    return total[: rows // 2], total[rows // 2 :]


def weight_grad(piece, rows, half, p, into, across):
    quarter = piece.shape[1]
    at = (half * 2 + p) * quarter
    if across:
        out = jnp.dot(rows, piece, preferred_element_type=f32).astype(bf16)
        return lax.dynamic_update_slice(into, out, (0, at))
    out = lax.dot_general(piece, rows, (((0,), (0,)), ((), ())), preferred_element_type=f32).astype(bf16)
    return lax.dynamic_update_slice(into, out, (at, 0))


def make(n_row, n_col):
    row_bits = n_row.bit_length() - 1
    col_bits = n_col.bit_length() - 1
    first = tuple(range(1, row_bits))
    orders = (first, first[::-1])
    steps = len(first)

    def swap_core(v):
        return lax.ppermute(v, "row", [(i, i ^ 1) for i in range(n_row)])

    def swap_chip(v, step):
        return lax.ppermute(v, "row", [(i, i ^ (1 << orders[i & 1][step])) for i in range(n_row)])

    def part(v, axis, index):
        return lax.slice_in_dim(v, index, index + 1, axis=axis)

    def flips(v, order, axis):
        me = lax.axis_index("row")
        for k, bit in enumerate(order):
            v = jnp.where((me >> bit) & 1 == 1, jnp.flip(v, axis + k), v)
        return v

    def relative(v):
        v = v.reshape((2,) * steps + (1, v.shape[0] >> steps, v.shape[1]))
        return flips(v, first, 0)

    def turn(v):
        return v.transpose(tuple(range(steps))[::-1] + tuple(range(steps, v.ndim)))

    def after(v, *tokens):
        return lax.optimization_barrier((v,) + tokens)[0]

    def flat(v):
        return v.reshape(-1, v.shape[-1])

    def per_device(latents, w_in, w_out, cotangent):
        tokens, width = latents.shape
        cut = w_in.shape[1] // 2
        core = lax.axis_index("row") & 1
        own_half = core.astype(jnp.int32)
        other_half = 1 - own_half

        taken = []

        def take(got, *also):
            got = after(got, *taken, *also)
            taken[:] = [got]
            return got

        def ordered(v):
            plain, turned = flat(v), flat(turn(v))
            return jnp.where(core == 0, plain, turned), jnp.where(core == 0, turned, plain)

        def by_core(parts):
            own = jnp.where(core == 0, parts[0], parts[1])
            return own, swap_core(jnp.where(core == 0, parts[1], parts[0]))

        def up(x):
            return by_core(
                [
                    jnp.dot(v, w_in[:, h * cut : (h + 1) * cut], preferred_element_type=f32).astype(bf16)
                    for h, v in enumerate((flat(x), flat(turn(x))))
                ]
            )

        def back(c):
            dims = (((1,), (1,)), ((), ()))
            return by_core(
                [
                    lax.dot_general(v, w_out[h * cut : (h + 1) * cut], dims, preferred_element_type=f32).astype(bf16)
                    for h, v in enumerate((flat(c), flat(turn(c))))
                ]
            )

        def step(keep, got, k):
            keep, send = add_and_split(keep, got)
            return keep, swap_chip(send, k)

        def total(keep, got):
            return (keep.astype(f32) + got.astype(f32)).reshape((1,) * steps + (-1, tokens >> steps, cut))

        def steps_on(flight, begin, end):
            for k in range(begin, end):
                flight = step(flight[0], take(flight[1]), k)
            return flight

        def reach(v, distance):
            return lax.ppermute(v, "col", [(i, i ^ distance) for i in range(n_col)])

        x_own, c_own = relative(latents), relative(cotangent)
        near = take(reach(lax.concatenate([x_own, c_own], steps + 2), 1))
        x_near = lax.concatenate([x_own, near[..., :width]], steps)
        c_near = lax.concatenate([c_own, near[..., width:]], steps)
        hid_near, grad_near = up(x_near), back(c_near)
        hid_near = step(hid_near[0], take(hid_near[1]), 0)
        grad_near = step(grad_near[0], take(grad_near[1]), 0)
        hid_near = hid_near[0], take(hid_near[1])
        x_far = lax.concatenate([take(reach(x_own, d)) for d in range(2, n_col)], steps)
        c_far = [reach(after(c_own, x_far), d) for d in range(2, n_col)]
        grad_near = grad_near[0], take(grad_near[1])
        x_far = after(x_far, grad_near[1])
        hid_near = step(*hid_near, 1)
        grad_near = step(*grad_near, 1)
        hid_far = up(x_far)
        hid_far = step(hid_far[0], take(hid_far[1]), 0)
        hid_near = steps_on(hid_near, 2, steps)
        hids = [total(hid_near[0], take(hid_near[1]))]
        x_all = lax.concatenate([x_near, x_far], steps)
        x_rows = [lax.optimization_barrier(v.T) for v in ordered(x_all)]
        grad_near = steps_on(grad_near, 2, steps)
        grads = [total(grad_near[0], take(grad_near[1], *x_rows))]
        c_far = lax.concatenate([take(v) for v in c_far], steps)
        hid_far = steps_on(hid_far, 1, steps)
        hid_far = hid_far[0], take(hid_far[1])
        hids.append(total(*hid_far))
        c_far = after(c_far, hid_far[1])
        c_all = lax.concatenate([c_near, c_far], steps)
        c_rows = [lax.optimization_barrier(v) for v in ordered(c_all)]
        grad_far = back(c_far)
        hid = lax.concatenate(hids, steps)
        act = gelu_parts(hid)[0].astype(bf16)

        def doubled(flight, k):
            return lax.concatenate([flight[0], take(flight[1])], k)

        def chips(v, begin, end):
            flight = v, swap_chip(v, end - 1)
            for k in reversed(range(begin, end - 1)):
                v = doubled(flight, k + 1)
                flight = v, swap_chip(v, k)
            return flight

        quarter = cut // 2

        def quarters(v):
            return [v[..., p * quarter : (p + 1) * quarter] for p in range(2)]

        act = chips(act, 1, steps)
        grad_far = step(grad_far[0], take(grad_far[1]), 0)
        grad_far = grad_far[0], take(grad_far[1], *c_rows)
        act = quarters(doubled(act, 1))
        grad_far = step(*grad_far, 1)
        acts = [(v, swap_chip(v, 0)) for v in act]
        grad_far = steps_on(grad_far, 2, steps)
        grads.append(total(grad_far[0], take(grad_far[1])))
        grad = lax.concatenate(grads, steps)
        hid, grad = lax.optimization_barrier((hid, grad))
        grad = chips((grad * gelu_parts(hid)[1]).astype(bf16), 1, steps)
        acts = [doubled(v, 0) for v in acts]
        acts = [(v, swap_core(v)) for v in acts]
        grad_w_out = jnp.zeros_like(w_out)
        for p in range(2):
            grad_w_out = weight_grad(flat(acts[p][0]), c_rows[0], own_half, p, grad_w_out, False)
        grad = grad[0], take(grad[1], grad_w_out)
        grad = quarters(lax.concatenate(grad, 1))
        grads = [(v, swap_chip(v, 0)) for v in grad]
        acts = [(v, take(got)) for v, got in acts]

        sums = []
        for i, half in enumerate((own_half, other_half)):
            parts = []
            for p in range(2):
                w = lax.dynamic_slice_in_dim(w_out, (half * 2 + p) * quarter, quarter, 0)
                parts.append(jnp.dot(flat(acts[p][i]), w, preferred_element_type=f32))
            sums.append((parts[0] + parts[1]).reshape(x_all.shape))
        mixed = jnp.where(core == 0, sums[0], sums[1]) + turn(jnp.where(core == 0, sums[1], sums[0]))
        mixed = mixed.astype(bf16)

        def halve(mixed, bit):
            blocks = mixed.shape[steps]
            mixed = mixed.reshape(mixed.shape[:steps] + (blocks // 2, 2) + mixed.shape[steps + 1 :])
            return (
                lax.index_in_dim(mixed, 0, steps + 1, False),
                reach(lax.index_in_dim(mixed, 1, steps + 1, False), 1 << bit),
            )

        def merged(flight, *also):
            return (flight[0].astype(f32) + take(flight[1], *also).astype(f32)).astype(bf16)

        for p in range(2):
            grad_w_out = weight_grad(flat(acts[p][1]), c_rows[1], other_half, p, grad_w_out, False)
        grads[0] = grads[0][0], take(grads[0][1], mixed, grad_w_out)
        mixed = halve(mixed, 0)
        mixed = merged(mixed)
        grads[0] = lax.concatenate([grads[0][0], after(grads[0][1], mixed)], 0)
        grads[0] = grads[0], swap_core(grads[0])
        grad_w_in = weight_grad(flat(grads[0][0]), x_rows[0], own_half, 0, jnp.zeros_like(w_in), True)
        for bit in range(1, col_bits):
            mixed = halve(mixed if bit == 1 else merged(mixed), bit)
        grads[1] = lax.concatenate([grads[1][0], take(grads[1][1], grad_w_in)], 0)
        grads[1] = grads[1], swap_core(grads[1])
        grads[0] = grads[0][0], take(grads[0][1])
        for p, i in ((0, 1), (1, 0)):
            grad_w_in = weight_grad(flat(grads[p][i]), x_rows[i], (own_half, other_half)[i], p, grad_w_in, True)
        grad_w_in = weight_grad(flat(take(grads[1][1])), x_rows[1], other_half, 1, grad_w_in, True)
        mixed = merged(mixed, grad_w_in) if col_bits > 1 else mixed
        mixed = flips(mixed, first, 0).reshape(tokens, width)
        return (mixed, grad_w_in, grad_w_out)

    return per_device


def solution(mesh):
    placed = (P("col", "row"), P("row", "col"), P("col", "row"), P("col", "row"))
    return jax.shard_map(
        make(mesh.shape["row"], mesh.shape["col"]),
        mesh=mesh,
        in_specs=placed,
        out_specs=(P("col", "row"), P("row", "col"), P("col", "row")),
        check_vma=False,
    )
```

profile of v0, /device:TPU:0, one launch (start us, length us, event | category | flops | bytes accessed | tf_op | source)
XLA Modules:
  0.0 198.4 jit_solution(12755234438232224926)
XLA Ops:
  2.9 3.1 %collective-permute-start = (bf16[2,2,1,32,1536]{4,3,2,1,0:T(8,128)(2,1)S(1)}, bf16[2,2,1,32,1536]{4,3,2,1,0:T(8,128)(2,1)S(1)}, u32[]{:S(2)}, u32[]{:S(2)}) collective-permute-start(bf16[2,2,1,32,1536]{4,3,2,1,0:T(8,128)(2,1)S(1)} %pad_maximum_fusion.10), channel_id=1, source_target_pairs={{0,1},{1,0},{2,3},{3,2},{4,5},{5,4},{6,7},{7,6},{8,9},{9,8},{10,11... | collective-permute-start | bytes 1179656 | tf_op jit(solution)/shard_map/ppermute | solution.py:119
  6.0 9.1 %collective-permute-done = bf16[2,2,1,32,1536]{4,3,2,1,0:T(8,128)(2,1)S(1)} collective-permute-done((bf16[2,2,1,32,1536]{4,3,2,1,0:T(8,128)(2,1)S(1)}, bf16[2,2,1,32,1536]{4,3,2,1,0:T(8,128)(2,1)S(1)}, u32[]{:S(2)}, u32[]{:S(2)}) %collective-permute-start) | collective-permute-done | bytes 393248 | tf_op jit(solution)/shard_map/ppermute | solution.py:119
  15.3 3.9 %fusion.16 = bf16[256,3072]{1,0:T(8,128)(2,1)S(1)} fusion(bf16[256,768]{1,0:T(8,128)(2,1)S(1)} %bitcast.130, bf16[768,6144]{1,0:T(8,128)(2,1)} %param.5), kind=kOutput, calls=%fused_computation.16 | convolution fusion | flops 1208745984 | bytes 6684672 | tf_op jit(solution)/shard_map/dot_general | solution.py:92
  26.2 3.4 %collective-permute-done.3 = bf16[256,3072]{1,0:T(8,128)(2,1)S(1)} collective-permute-done((bf16[256,3072]{1,0:T(8,128)(2,1)S(1)}, bf16[256,3072]{1,0:T(8,128)(2,1)S(1)}, u32[]{:S(2)}, u32[]{:S(2)}) %collective-permute-start.3) | collective-permute-done | bytes 1572896 | tf_op jit(solution)/shard_map/ppermute | solution.py:40
  33.5 2.8 %collective-permute-start.5 = (bf16[2,2,1,32,768]{4,3,2,1,0:T(8,128)(2,1)S(1)}, bf16[2,2,1,32,768]{4,3,2,1,0:T(8,128)(2,1)S(1)}, u32[]{:S(2)}, u32[]{:S(2)}) collective-permute-start(bf16[2,2,1,32,768]{4,3,2,1,0:T(8,128)(2,1)S(1)} %reverse_select_fusion.4), channel_id=1, source_target_pairs={{0,2},{1,3},{2,0},{3,1},{4,6},{5,7},{6,4},{7,5},{8,10},{9,11},{10,... | collective-permute-start | bytes 589832 | tf_op jit(solution)/shard_map/ppermute | solution.py:119
  37.6 4.9 %collective-permute-done.2 = bf16[128,3072]{1,0:T(8,128)(2,1)S(1)} collective-permute-done((bf16[128,3072]{1,0:T(8,128)(2,1)S(1)}, bf16[128,3072]{1,0:T(8,128)(2,1)S(1)}, u32[]{:S(2)}, u32[]{:S(2)}) %collective-permute-start.2) | collective-permute-done | bytes 786464 | tf_op jit(solution)/shard_map/ppermute | solution.py:43
  42.5 8.0 %collective-permute-done.5 = bf16[2,2,1,32,768]{4,3,2,1,0:T(8,128)(2,1)S(1)} collective-permute-done((bf16[2,2,1,32,768]{4,3,2,1,0:T(8,128)(2,1)S(1)}, bf16[2,2,1,32,768]{4,3,2,1,0:T(8,128)(2,1)S(1)}, u32[]{:S(2)}, u32[]{:S(2)}) %collective-permute-start.5) | collective-permute-done | bytes 196640 | tf_op jit(solution)/shard_map/ppermute | solution.py:119
  54.0 5.3 %collective-permute-start.11 = (bf16[2,2,1,32,768]{4,3,2,1,0:T(8,128)(2,1)S(1)}, bf16[2,2,1,32,768]{4,3,2,1,0:T(8,128)(2,1)S(1)}, u32[]{:S(2)}, u32[]{:S(2)}) collective-permute-start(bf16[2,2,1,32,768]{4,3,2,1,0:T(8,128)(2,1)S(1)} %reverse_select_fusion.2), channel_id=1, source_target_pairs={{0,2},{1,3},{2,0},{3,1},{4,6},{5,7},{6,4},{7,5},{8,10},{9,11},{10,... | collective-permute-start | bytes 589832 | tf_op jit(solution)/shard_map/ppermute | solution.py:119
  66.1 4.9 %collective-permute-done.4 = bf16[64,3072]{1,0:T(8,128)(2,1)S(1)} collective-permute-done((bf16[64,3072]{1,0:T(8,128)(2,1)S(1)}, bf16[64,3072]{1,0:T(8,128)(2,1)S(1)}, u32[]{:S(2)}, u32[]{:S(2)}) %collective-permute-start.4) | collective-permute-done | bytes 393248 | tf_op jit(solution)/shard_map/ppermute | solution.py:43
  71.0 8.4 %collective-permute-done.12 = bf16[64,3072]{1,0:T(8,128)(2,1)S(1)} collective-permute-done((bf16[64,3072]{1,0:T(8,128)(2,1)S(1)}, bf16[64,3072]{1,0:T(8,128)(2,1)S(1)}, u32[]{:S(2)}, u32[]{:S(2)}) %collective-permute-start.12) | collective-permute-done | bytes 393248 | tf_op jit(solution)/shard_map/ppermute | solution.py:43
  81.7 6.2 %collective-permute-done.13 = bf16[64,3072]{1,0:T(8,128)(2,1)S(1)} collective-permute-done((bf16[64,3072]{1,0:T(8,128)(2,1)S(1)}, bf16[64,3072]{1,0:T(8,128)(2,1)S(1)}, u32[]{:S(2)}, u32[]{:S(2)}) %collective-permute-start.13) | collective-permute-done | bytes 393248 | tf_op jit(solution)/shard_map/ppermute | solution.py:43
  90.4 3.1 %broadcast_select_fusion = (bf16[256,3072]{1,0:T(8,128)(2,1)}, bf16[256,3072]{1,0:T(8,128)(2,1)}) fusion(bf16[256,3072]{1,0:T(8,128)(2,1)S(1)} %fusion.37, pred[]{:T(512)S(6)} %eq.8, bf16[256,768]{1,0:T(8,128)(2,1)S(1)} %bitcast.135, bf16[6144,768]{1,0:T(8,128)(2,1)S(1)} %bitcast.126), kind=kOutput, calls=%fused_computation.76 | convolution fusion | flops 1209532416 | bytes 9830401 | tf_op jit(solution)/shard_map/dot_general | solution.py:101
  99.5 2.5 %collective-permute-start.16 = (bf16[128,3072]{1,0:T(8,128)(2,1)S(1)}, bf16[128,3072]{1,0:T(8,128)(2,1)S(1)}, u32[]{:S(2)}, u32[]{:S(2)}) collective-permute-start(bf16[128,3072]{1,0:T(8,128)(2,1)S(1)} %slice.137), channel_id=1, source_target_pairs={{0,8},{4,20},{8,0},{12,28},{16,24},{20,4},{24,16},{28,12},{1,9},{5... | collective-permute-start | bytes 2359304 | tf_op jit(solution)/shard_map/ppermute | solution.py:43
  104.1 15.1 %collective-permute-done.16 = bf16[128,3072]{1,0:T(8,128)(2,1)S(1)} collective-permute-done((bf16[128,3072]{1,0:T(8,128)(2,1)S(1)}, bf16[128,3072]{1,0:T(8,128)(2,1)S(1)}, u32[]{:S(2)}, u32[]{:S(2)}) %collective-permute-start.16) | collective-permute-done | bytes 786464 | tf_op jit(solution)/shard_map/ppermute | solution.py:43
  121.7 2.4 %collective-permute-start.17 = (bf16[1,2,4,32,1536]{4,3,2,1,0:T(8,128)(2,1)S(1)}, bf16[1,2,4,32,1536]{4,3,2,1,0:T(8,128)(2,1)S(1)}, u32[]{:S(2)}, u32[]{:S(2)}) collective-permute-start(bf16[1,2,4,32,1536]{4,3,2,1,0:T(8,128)(2,1)S(1)} %get-tuple-element.77), channel_id=1, source_target_pairs={{0,8},{4,20},{8,0},{12,28},{16,24},{20,4},{24,16},{28,12},{1,9},{5... | collective-permute-start | bytes 2359304 | tf_op jit(solution)/shard_map/ppermute | solution.py:43
  124.1 7.3 %collective-permute-done.18 = bf16[64,3072]{1,0:T(8,128)(2,1)S(1)} collective-permute-done((bf16[64,3072]{1,0:T(8,128)(2,1)S(1)}, bf16[64,3072]{1,0:T(8,128)(2,1)S(1)}, u32[]{:S(2)}, u32[]{:S(2)}) %collective-permute-start.18) | collective-permute-done | bytes 393248 | tf_op jit(solution)/shard_map/ppermute | solution.py:43
  134.3 5.2 %collective-permute-done.17 = bf16[1,2,4,32,1536]{4,3,2,1,0:T(8,128)(2,1)S(1)} collective-permute-done((bf16[1,2,4,32,1536]{4,3,2,1,0:T(8,128)(2,1)S(1)}, bf16[1,2,4,32,1536]{4,3,2,1,0:T(8,128)(2,1)S(1)}, u32[]{:S(2)}, u32[]{:S(2)}) %collective-permute-start.17) | collective-permute-done | bytes 786464 | tf_op jit(solution)/shard_map/ppermute | solution.py:43
  139.6 11.3 %collective-permute-done.19 = bf16[1,2,4,32,1536]{4,3,2,1,0:T(8,128)(2,1)S(1)} collective-permute-done((bf16[1,2,4,32,1536]{4,3,2,1,0:T(8,128)(2,1)S(1)}, bf16[1,2,4,32,1536]{4,3,2,1,0:T(8,128)(2,1)S(1)}, u32[]{:S(2)}, u32[]{:S(2)}) %collective-permute-start.19) | collective-permute-done | bytes 786464 | tf_op jit(solution)/shard_map/ppermute | solution.py:43
  169.7 3.6 %collective-permute-done.24 = bf16[1,2,4,32,1536]{4,3,2,1,0:T(8,128)(2,1)S(1)} collective-permute-done((bf16[1,2,4,32,1536]{4,3,2,1,0:T(8,128)(2,1)S(1)}, bf16[1,2,4,32,1536]{4,3,2,1,0:T(8,128)(2,1)S(1)}, u32[]{:S(2)}, u32[]{:S(2)}) %collective-permute-start.24) | collective-permute-done | bytes 786464 | tf_op jit(solution)/shard_map/ppermute | solution.py:43
  173.4 4.4 %collective-permute-done.23 = bf16[2,2,2,32,768]{4,3,1,0,2:T(8,128)(2,1)S(1)} collective-permute-done((bf16[2,2,2,32,768]{4,3,1,0,2:T(8,128)(2,1)S(1)}, bf16[2,2,2,32,768]{4,3,1,0,2:T(8,128)(2,1)S(1)}, u32[]{:S(2)}, u32[]{:S(2)}) %collective-permute-start.23) | collective-permute-done | bytes 393248 | tf_op jit(solution)/shard_map/ppermute | solution.py:119
  180.3 3.1 %fusion.43 = bf16[768,6144]{1,0:T(8,128)(2,1)S(1)} fusion(bf16[768,6144]{1,0:T(8,128)(2,1)S(1)} %broadcast_in_dim.7, s32[]{:T(128)S(6)} %select_n.161, bf16[768,512]{0,1:T(8,128)(2,1)} %bitcast.119, bf16[512,1536]{1,0:T(8,128)(2,1)} %bitcast.40), kind=kOutput, calls=%fused_computation.31 | convolution fusion | flops 1209139200 | bytes 4718596 | tf_op jit(solution)/shard_map/dot_general | solution.py:26
  185.6 2.3 %collective-permute-start.25 = (bf16[2,2,1,32,768]{4,3,2,1,0:T(8,128)(2,1)S(1)}, bf16[2,2,1,32,768]{4,3,2,1,0:T(8,128)(2,1)S(1)}, u32[]{:S(2)}, u32[]{:S(2)}) collective-permute-start(bf16[2,2,1,32,768]{4,3,2,1,0:T(8,128)(2,1)S(1)} %slice_bitcast_fusion), channel_id=1, source_target_pairs={{0,2},{1,3},{2,0},{3,1},{4,6},{5,7},{6,4},{7,5},{8,10},{9,11},{10,... | collective-permute-start | bytes 589832 | tf_op jit(solution)/shard_map/ppermute | solution.py:119
  187.8 2.9 %fusion.42 = bf16[768,6144]{1,0:T(8,128)(2,1)S(1)} fusion(bf16[768,6144]{1,0:T(8,128)(2,1)S(1)} %fusion.43, s32[]{:T(128)S(6)} %select_n.163, bf16[768,512]{0,1:T(8,128)(2,1)S(1)} %bitcast.117, bf16[512,1536]{1,0:T(8,128)(2,1)} %bitcast.41), kind=kOutput, calls=%fused_computation.29 | convolution fusion | flops 1209139200 | bytes 4718596 | tf_op jit(solution)/shard_map/dot_general | solution.py:26
  193.6 3.9 %collective-permute-done.25 = bf16[2,2,1,32,768]{4,3,2,1,0:T(8,128)(2,1)S(1)} collective-permute-done((bf16[2,2,1,32,768]{4,3,2,1,0:T(8,128)(2,1)S(1)}, bf16[2,2,1,32,768]{4,3,2,1,0:T(8,128)(2,1)S(1)}, u32[]{:S(2)}, u32[]{:S(2)}) %collective-permute-start.25) | collective-permute-done | bytes 196640 | tf_op jit(solution)/shard_map/ppermute | solution.py:119
  (153 shorter events, 69.9 us)
Async XLA Ops:
  2.9 12.2 %collective-permute-start = (bf16[2,2,1,32,1536]{4,3,2,1,0:T(8,128)(2,1)S(1)}, bf16[2,2,1,32,1536]{4,3,2,1,0:T(8,128)(2,1)S(1)}, u32[]{:S(2)}, u32[]{:S(2)}) collective-permute-start(bf16[2,2,1,32,1536]{4,3,2,1,0:T(8,128)(2,1)S(1)} %pad_maximum_fusion.10), channel_id=1, source_target_pairs={{0,1},{1,0},{2,3},{3,2},{4,5},{5,4},{6,7},{7,6},{8,9},{9,8},{10,11... | collective-permute-start | bytes 1179656 | tf_op jit(solution)/shard_map/ppermute | solution.py:119
  30.5 12.1 %collective-permute-start.2 = (bf16[128,3072]{1,0:T(8,128)(2,1)S(1)}, bf16[128,3072]{1,0:T(8,128)(2,1)S(1)}, u32[]{:S(2)}, u32[]{:S(2)}) collective-permute-start(bf16[128,3072]{1,0:T(8,128)(2,1)S(1)} %slice.126), channel_id=1, source_target_pairs={{0,8},{4,20},{8,0},{12,28},{16,24},{20,4},{24,16},{28,12},{1,9},{5... | collective-permute-start | bytes 2359304 | tf_op jit(solution)/shard_map/ppermute | solution.py:43
  33.0 17.9 %collective-permute-start.7 = (bf16[128,3072]{1,0:T(8,128)(2,1)S(1)}, bf16[128,3072]{1,0:T(8,128)(2,1)S(1)}, u32[]{:S(2)}, u32[]{:S(2)}) collective-permute-start(bf16[128,3072]{1,0:T(8,128)(2,1)S(1)} %slice.130), channel_id=1, source_target_pairs={{0,8},{4,20},{8,0},{12,28},{16,24},{20,4},{24,16},{28,12},{1,9},{5... | collective-permute-start | bytes 2359304 | tf_op jit(solution)/shard_map/ppermute | solution.py:43
  33.5 17.0 %collective-permute-start.5 = (bf16[2,2,1,32,768]{4,3,2,1,0:T(8,128)(2,1)S(1)}, bf16[2,2,1,32,768]{4,3,2,1,0:T(8,128)(2,1)S(1)}, u32[]{:S(2)}, u32[]{:S(2)}) collective-permute-start(bf16[2,2,1,32,768]{4,3,2,1,0:T(8,128)(2,1)S(1)} %reverse_select_fusion.4), channel_id=1, source_target_pairs={{0,2},{1,3},{2,0},{3,1},{4,6},{5,7},{6,4},{7,5},{8,10},{9,11},{10,... | collective-permute-start | bytes 589832 | tf_op jit(solution)/shard_map/ppermute | solution.py:119
  36.2 14.3 %collective-permute-start.6 = (bf16[2,2,1,32,768]{4,3,2,1,0:T(8,128)(2,1)S(1)}, bf16[2,2,1,32,768]{4,3,2,1,0:T(8,128)(2,1)S(1)}, u32[]{:S(2)}, u32[]{:S(2)}) collective-permute-start(bf16[2,2,1,32,768]{4,3,2,1,0:T(8,128)(2,1)S(1)} %reverse_select_fusion.4), channel_id=1, source_target_pairs={{0,3},{1,2},{2,1},{3,0},{4,7},{5,6},{6,5},{7,4},{8,11},{9,10},{10,... | collective-permute-start | bytes 589832 | tf_op jit(solution)/shard_map/ppermute | solution.py:119
  54.0 25.4 %collective-permute-start.11 = (bf16[2,2,1,32,768]{4,3,2,1,0:T(8,128)(2,1)S(1)}, bf16[2,2,1,32,768]{4,3,2,1,0:T(8,128)(2,1)S(1)}, u32[]{:S(2)}, u32[]{:S(2)}) collective-permute-start(bf16[2,2,1,32,768]{4,3,2,1,0:T(8,128)(2,1)S(1)} %reverse_select_fusion.2), channel_id=1, source_target_pairs={{0,2},{1,3},{2,0},{3,1},{4,6},{5,7},{6,4},{7,5},{8,10},{9,11},{10,... | collective-permute-start | bytes 589832 | tf_op jit(solution)/shard_map/ppermute | solution.py:119
  59.3 20.1 %collective-permute-start.10 = (bf16[2,2,1,32,768]{4,3,2,1,0:T(8,128)(2,1)S(1)}, bf16[2,2,1,32,768]{4,3,2,1,0:T(8,128)(2,1)S(1)}, u32[]{:S(2)}, u32[]{:S(2)}) collective-permute-start(bf16[2,2,1,32,768]{4,3,2,1,0:T(8,128)(2,1)S(1)} %reverse_select_fusion.2), channel_id=1, source_target_pairs={{0,3},{1,2},{2,1},{3,0},{4,7},{5,6},{6,5},{7,4},{8,11},{9,10},{10,... | collective-permute-start | bytes 589832 | tf_op jit(solution)/shard_map/ppermute | solution.py:119
  60.0 11.0 %collective-permute-start.4 = (bf16[64,3072]{1,0:T(8,128)(2,1)S(1)}, bf16[64,3072]{1,0:T(8,128)(2,1)S(1)}, u32[]{:S(2)}, u32[]{:S(2)}) collective-permute-start(bf16[64,3072]{1,0:T(8,128)(2,1)S(1)} %slice.129), channel_id=1, source_target_pairs={{0,16},{4,12},{8,24},{12,4},{16,0},{20,28},{24,8},{28,20},{1,17},{... | collective-permute-start | bytes 1179656 | tf_op jit(solution)/shard_map/ppermute | solution.py:43
  62.4 17.0 %collective-permute-start.9 = (bf16[128,3072]{1,0:T(8,128)(2,1)S(1)}, bf16[128,3072]{1,0:T(8,128)(2,1)S(1)}, u32[]{:S(2)}, u32[]{:S(2)}) collective-permute-start(bf16[128,3072]{1,0:T(8,128)(2,1)S(1)} %slice.132), channel_id=1, source_target_pairs={{0,8},{4,20},{8,0},{12,28},{16,24},{20,4},{24,16},{28,12},{1,9},{5... | collective-permute-start | bytes 2359304 | tf_op jit(solution)/shard_map/ppermute | solution.py:43
  64.2 15.2 %collective-permute-start.12 = (bf16[64,3072]{1,0:T(8,128)(2,1)S(1)}, bf16[64,3072]{1,0:T(8,128)(2,1)S(1)}, u32[]{:S(2)}, u32[]{:S(2)}) collective-permute-start(bf16[64,3072]{1,0:T(8,128)(2,1)S(1)} %slice.134), channel_id=1, source_target_pairs={{0,16},{4,12},{8,24},{12,4},{16,0},{20,28},{24,8},{28,20},{1,17},{... | collective-permute-start | bytes 1179656 | tf_op jit(solution)/shard_map/ppermute | solution.py:43
  80.2 7.8 %collective-permute-start.13 = (bf16[64,3072]{1,0:T(8,128)(2,1)S(1)}, bf16[64,3072]{1,0:T(8,128)(2,1)S(1)}, u32[]{:S(2)}, u32[]{:S(2)}) collective-permute-start(bf16[64,3072]{1,0:T(8,128)(2,1)S(1)} %slice.136), channel_id=1, source_target_pairs={{0,16},{4,12},{8,24},{12,4},{16,0},{20,28},{24,8},{28,20},{1,17},{... | collective-permute-start | bytes 1179656 | tf_op jit(solution)/shard_map/ppermute | solution.py:43
  99.5 19.7 %collective-permute-start.16 = (bf16[128,3072]{1,0:T(8,128)(2,1)S(1)}, bf16[128,3072]{1,0:T(8,128)(2,1)S(1)}, u32[]{:S(2)}, u32[]{:S(2)}) collective-permute-start(bf16[128,3072]{1,0:T(8,128)(2,1)S(1)} %slice.137), channel_id=1, source_target_pairs={{0,8},{4,20},{8,0},{12,28},{16,24},{20,4},{24,16},{28,12},{1,9},{5... | collective-permute-start | bytes 2359304 | tf_op jit(solution)/shard_map/ppermute | solution.py:43
  102.5 19.0 %collective-permute-start.14 = (bf16[1,1,4,32,3072]{4,3,2,1,0:T(8,128)(2,1)S(1)}, bf16[1,1,4,32,3072]{4,3,2,1,0:T(8,128)(2,1)S(1)}, u32[]{:S(2)}, u32[]{:S(2)}) collective-permute-start(bf16[1,1,4,32,3072]{4,3,2,1,0:T(8,128)(2,1)S(1)} %get-tuple-element.76), channel_id=1, source_target_pairs={{0,16},{4,12},{8,24},{12,4},{16,0},{20,28},{24,8},{28,20},{1,17},{... | collective-permute-start | bytes 2359304 | tf_op jit(solution)/shard_map/ppermute | solution.py:43
  119.4 12.1 %collective-permute-start.18 = (bf16[64,3072]{1,0:T(8,128)(2,1)S(1)}, bf16[64,3072]{1,0:T(8,128)(2,1)S(1)}, u32[]{:S(2)}, u32[]{:S(2)}) collective-permute-start(bf16[64,3072]{1,0:T(8,128)(2,1)S(1)} %slice.141), channel_id=1, source_target_pairs={{0,16},{4,12},{8,24},{12,4},{16,0},{20,28},{24,8},{28,20},{1,17},{... | collective-permute-start | bytes 1179656 | tf_op jit(solution)/shard_map/ppermute | solution.py:43
  121.7 17.8 %collective-permute-start.17 = (bf16[1,2,4,32,1536]{4,3,2,1,0:T(8,128)(2,1)S(1)}, bf16[1,2,4,32,1536]{4,3,2,1,0:T(8,128)(2,1)S(1)}, u32[]{:S(2)}, u32[]{:S(2)}) collective-permute-start(bf16[1,2,4,32,1536]{4,3,2,1,0:T(8,128)(2,1)S(1)} %get-tuple-element.77), channel_id=1, source_target_pairs={{0,8},{4,20},{8,0},{12,28},{16,24},{20,4},{24,16},{28,12},{1,9},{5... | collective-permute-start | bytes 2359304 | tf_op jit(solution)/shard_map/ppermute | solution.py:43
  124.1 26.8 %collective-permute-start.19 = (bf16[1,2,4,32,1536]{4,3,2,1,0:T(8,128)(2,1)S(1)}, bf16[1,2,4,32,1536]{4,3,2,1,0:T(8,128)(2,1)S(1)}, u32[]{:S(2)}, u32[]{:S(2)}) collective-permute-start(bf16[1,2,4,32,1536]{4,3,2,1,0:T(8,128)(2,1)S(1)} %get-tuple-element.78), channel_id=1, source_target_pairs={{0,8},{4,20},{8,0},{12,28},{16,24},{20,4},{24,16},{28,12},{1,9},{5... | collective-permute-start | bytes 2359304 | tf_op jit(solution)/shard_map/ppermute | solution.py:43
  132.3 28.0 %collective-permute-start.21 = (bf16[1,1,4,32,3072]{4,3,2,1,0:T(8,128)(2,1)S(1)}, bf16[1,1,4,32,3072]{4,3,2,1,0:T(8,128)(2,1)S(1)}, u32[]{:S(2)}, u32[]{:S(2)}) collective-permute-start(bf16[1,1,4,32,3072]{4,3,2,1,0:T(8,128)(2,1)S(1)} %fusion.61), channel_id=1, source_target_pairs={{0,16},{4,12},{8,24},{12,4},{16,0},{20,28},{24,8},{28,20},{1,17},{... | collective-permute-start | bytes 2359304 | tf_op jit(solution)/shard_map/ppermute | solution.py:43
  151.0 12.4 %collective-permute-start.20 = (bf16[2,2,4,32,1536]{4,3,2,1,0:T(8,128)(2,1)S(1)}, bf16[2,2,4,32,1536]{4,3,2,1,0:T(8,128)(2,1)S(1)}, u32[]{:S(2)}, u32[]{:S(2)}) collective-permute-start(bf16[2,2,4,32,1536]{4,3,2,1,0:T(8,128)(2,1)S(1)} %pad_maximum_fusion.1), channel_id=1, source_target_pairs={{0,4},{4,0},{8,12},{12,8},{16,20},{20,16},{24,28},{28,24},{1,5},{5... | collective-permute-start | bytes 4718600 | tf_op jit(solution)/shard_map/ppermute | solution.py:40
  152.5 10.9 %collective-permute-start.22 = (bf16[2,2,4,32,1536]{4,3,2,1,0:T(8,128)(2,1)S(1)}, bf16[2,2,4,32,1536]{4,3,2,1,0:T(8,128)(2,1)S(1)}, u32[]{:S(2)}, u32[]{:S(2)}) collective-permute-start(bf16[2,2,4,32,1536]{4,3,2,1,0:T(8,128)(2,1)S(1)} %pad_maximum_fusion.2), channel_id=1, source_target_pairs={{0,4},{4,0},{8,12},{12,8},{16,20},{20,16},{24,28},{28,24},{1,5},{5... | collective-permute-start | bytes 4718600 | tf_op jit(solution)/shard_map/ppermute | solution.py:40
  161.4 12.0 %collective-permute-start.24 = (bf16[1,2,4,32,1536]{4,3,2,1,0:T(8,128)(2,1)S(1)}, bf16[1,2,4,32,1536]{4,3,2,1,0:T(8,128)(2,1)S(1)}, u32[]{:S(2)}, u32[]{:S(2)}) collective-permute-start(bf16[1,2,4,32,1536]{4,3,2,1,0:T(8,128)(2,1)S(1)} %get-tuple-element.74), channel_id=1, source_target_pairs={{0,8},{4,20},{8,0},{12,28},{16,24},{20,4},{24,16},{28,12},{1,9},{5... | collective-permute-start | bytes 2359304 | tf_op jit(solution)/shard_map/ppermute | solution.py:43
  163.2 20.2 %collective-permute-start.26 = (bf16[1,2,4,32,1536]{4,3,2,1,0:T(8,128)(2,1)}, bf16[1,2,4,32,1536]{4,3,2,1,0:T(8,128)(2,1)}, u32[]{:S(2)}, u32[]{:S(2)}) collective-permute-start(bf16[1,2,4,32,1536]{4,3,2,1,0:T(8,128)(2,1)} %get-tuple-element.73), channel_id=1, source_target_pairs={{0,8},{4,20},{8,0},{12,28},{16,24},{20,4},{24,16},{28,12},{1,9},{5... | collective-permute-start | bytes 2359304 | tf_op jit(solution)/shard_map/ppermute | solution.py:43
  166.8 11.0 %collective-permute-start.23 = (bf16[2,2,2,32,768]{4,3,1,0,2:T(8,128)(2,1)S(1)}, bf16[2,2,2,32,768]{4,3,1,0,2:T(8,128)(2,1)S(1)}, u32[]{:S(2)}, u32[]{:S(2)}) collective-permute-start(bf16[2,2,2,32,768]{4,3,1,0,2:T(8,128)(2,1)S(1)} %bitcast.131), channel_id=1, source_target_pairs={{0,1},{1,0},{2,3},{3,2},{4,5},{5,4},{6,7},{7,6},{8,9},{9,8},{10,11... | collective-permute-start | bytes 1179656 | tf_op jit(solution)/shard_map/ppermute | solution.py:119
  179.1 8.7 %collective-permute-start.28 = (bf16[2,2,4,32,1536]{4,3,2,1,0:T(8,128)(2,1)}, bf16[2,2,4,32,1536]{4,3,2,1,0:T(8,128)(2,1)}, u32[]{:S(2)}, u32[]{:S(2)}) collective-permute-start(bf16[2,2,4,32,1536]{4,3,2,1,0:T(8,128)(2,1)} %pad_maximum_fusion.4), channel_id=1, source_target_pairs={{0,4},{4,0},{8,12},{12,8},{16,20},{20,16},{24,28},{28,24},{1,5},{5... | collective-permute-start | bytes 4718600 | tf_op jit(solution)/shard_map/ppermute | solution.py:40
  185.6 12.0 %collective-permute-start.25 = (bf16[2,2,1,32,768]{4,3,2,1,0:T(8,128)(2,1)S(1)}, bf16[2,2,1,32,768]{4,3,2,1,0:T(8,128)(2,1)S(1)}, u32[]{:S(2)}, u32[]{:S(2)}) collective-permute-start(bf16[2,2,1,32,768]{4,3,2,1,0:T(8,128)(2,1)S(1)} %slice_bitcast_fusion), channel_id=1, source_target_pairs={{0,2},{1,3},{2,0},{3,1},{4,6},{5,7},{6,4},{7,5},{8,10},{9,11},{10,... | collective-permute-start | bytes 589832 | tf_op jit(solution)/shard_map/ppermute | solution.py:119
  (25 other events, 128.1 us)
where the time goes:
time: 199 us; the launch traced here: 198 us
  waiting for transfers between devices  97.8 us (49%)
  starting transfers between devices  37.5 us (19%)
  matrix products  36.2 us (18%)
  other arithmetic  17.9 us (9%)
  local copies, waits for them, and re-layouts  7.61 us (4%)
    ppermute x14, waiting for transfers between devices, swap_chip(): lax.ppermute(v, 'row', [(i, i ^ 1 << orders[i & 1][step]) for i in range(...  67.5 us
    ppermute x7, waiting for transfers between devices, reach(): return lax.ppermute(v, 'col', [(i, i ^ distance) for i in range(n_col)])  25.4 us
    ppermute x14, starting transfers between devices, swap_chip(): lax.ppermute(v, 'row', [(i, i ^ 1 << orders[i & 1][step]) for i in range(...  19.9 us
    ppermute x7, starting transfers between devices, reach(): return lax.ppermute(v, 'col', [(i, i ^ distance) for i in range(n_col)])  15.3 us
    dot_general x4, matrix products, weight_grad(): out = jnp.dot(rows, piece, preferred_element_type=f32).astype(bf16)  8.82 us
    dot_general x4, matrix products, up(): jnp.dot(v, w_in[:, h * cut:(h + 1) * cut], preferred_element_type=f32)  8.28 us
    dot_general x4, matrix products, back(): lax.dot_general(v, w_out[h * cut:(h + 1) * cut], dims, preferred_element_...  7.62 us
    dot_general x4, matrix products, per_device(): parts.append(jnp.dot(flat(acts[p][i]), w, preferred_element_type=f32))  5.78 us
  transfers between devices with their start and end apart: 29, of which 16 were waited for; matrix products, arithmetic and copies ran while one was open for 19% of the time, Pallas kernels for 0%

commit v1 on v0

--- a/solution.py
+++ b/solution.py
@@ -141,13 +141,14 @@
         grad_near = steps_on(grad_near, 2, steps)
         grads = [total(grad_near[0], take(grad_near[1], *x_rows))]
         c_far = lax.concatenate([take(v) for v in c_far], steps)
-        hid_far = steps_on(hid_far, 1, steps)
         hid_far = hid_far[0], take(hid_far[1])
-        hids.append(total(*hid_far))
         c_far = after(c_far, hid_far[1])
         c_all = lax.concatenate([c_near, c_far], steps)
         c_rows = [lax.optimization_barrier(v) for v in ordered(c_all)]
         grad_far = back(c_far)
+        hid_far = step(*hid_far, 1)
+        hid_far = steps_on(hid_far, 2, steps)
+        hids.append(total(hid_far[0], take(hid_far[1])))
         hid = lax.concatenate(hids, steps)
         act = gelu_parts(hid)[0].astype(bf16)
 
@@ -177,23 +178,22 @@
         grad = lax.concatenate(grads, steps)
         hid, grad = lax.optimization_barrier((hid, grad))
         grad = chips((grad * gelu_parts(hid)[1]).astype(bf16), 1, steps)
-        acts = [doubled(v, 0) for v in acts]
-        acts = [(v, swap_core(v)) for v in acts]
-        grad_w_out = jnp.zeros_like(w_out)
-        for p in range(2):
-            grad_w_out = weight_grad(flat(acts[p][0]), c_rows[0], own_half, p, grad_w_out, False)
-        grad = grad[0], take(grad[1], grad_w_out)
-        grad = quarters(lax.concatenate(grad, 1))
+        def down(v, half, p):
+            w = lax.dynamic_slice_in_dim(w_out, (half * 2 + p) * quarter, quarter, 0)
+            return jnp.dot(flat(v), w, preferred_element_type=f32)
+
+        own = [doubled(acts[0], 0)]
+        got = [swap_core(own[0])]
+        grad_w_out = weight_grad(flat(own[0]), c_rows[0], own_half, 0, jnp.zeros_like(w_out), False)
+        grad = quarters(lax.concatenate([grad[0], take(grad[1], grad_w_out)], 1))
         grads = [(v, swap_chip(v, 0)) for v in grad]
-        acts = [(v, take(got)) for v, got in acts]
-
-        sums = []
-        for i, half in enumerate((own_half, other_half)):
-            parts = []
-            for p in range(2):
-                w = lax.dynamic_slice_in_dim(w_out, (half * 2 + p) * quarter, quarter, 0)
-                parts.append(jnp.dot(flat(acts[p][i]), w, preferred_element_type=f32))
-            sums.append((parts[0] + parts[1]).reshape(x_all.shape))
+        own.append(doubled(acts[1], 0))
+        got.append(swap_core(own[1]))
+        got = [take(v) for v in got]
+        sums = [
+            (down(v[0], half, 0) + down(v[1], half, 1)).reshape(x_all.shape)
+            for v, half in ((own, own_half), (got, other_half))
+        ]
         mixed = jnp.where(core == 0, sums[0], sums[1]) + turn(jnp.where(core == 0, sums[1], sums[0]))
         mixed = mixed.astype(bf16)
 
@@ -208,8 +208,12 @@
         def merged(flight, *also):
             return (flight[0].astype(f32) + take(flight[1], *also).astype(f32)).astype(bf16)
 
-        for p in range(2):
-            grad_w_out = weight_grad(flat(acts[p][1]), c_rows[1], other_half, p, grad_w_out, False)
+        for half, rows, v, p in (
+            (other_half, c_rows[1], got[0], 0),
+            (own_half, c_rows[0], own[1], 1),
+            (other_half, c_rows[1], got[1], 1),
+        ):
+            grad_w_out = weight_grad(flat(v), rows, half, p, grad_w_out, False)
         grads[0] = grads[0][0], take(grads[0][1], mixed, grad_w_out)
         mixed = halve(mixed, 0)
         mixed = merged(mixed)

time: 199 us -> 198 us (level)
  waiting for transfers between devices: 97.8 us -> 81.2 us
  matrix products: 36.2 us -> 49.9 us
    ppermute x14, waiting for transfers between devices: 67.5 us -> 50.8 us  [swap_chip(): lax.ppermute(v, 'row', [(i, i ^ 1 << orders[i & 1][step]) for i in range(...]
    dot_general x4, matrix products: 5.71 us -> 17.1 us  [weight_grad(): lax.dot_general(piece, rows, (((0,), (0,)), ((), ())), preferred_element_...]
    dot_general x4, matrix products: 5.78 us -> 13 us  [down(): return jnp.dot(flat(v), w, preferred_element_type=f32)]
    concatenate x3, other arithmetic: 0.39 us -> 5.02 us  [doubled(): return lax.concatenate([flight[0], take(flight[1])], k)]
    ppermute x7, starting transfers between devices: 15.3 us -> 19.8 us  [reach(): return lax.ppermute(v, 'col', [(i, i ^ distance) for i in range(n_col)])]
    broadcast_in_dim x1, local copies, waits for them, and re-layouts: 0.61 us -> 4.35 us  [per_device(): jnp.zeros_like(w_out)]
    dot_general x4, matrix products: 8.82 us -> 5.67 us  [weight_grad(): out = jnp.dot(rows, piece, preferred_element_type=f32).astype(bf16)]
    unnamed x42 -> x24, local copies, waits for them, and re-layouts: 5.31 us -> 2.49 us
  transfers between devices with their start and end apart: 29 -> 29, of which waited for: 16 -> 16; matrix products, arithmetic and copies ran while one was open for 19% -> 29% of each run, Pallas kernels for 0% -> 0%
where the time goes in v1:
time: 198 us; the launch traced here: 197 us
  waiting for transfers between devices  81.2 us (41%)
  matrix products  49.9 us (25%)
  starting transfers between devices  38.4 us (19%)
  other arithmetic  17.8 us (9%)
  local copies, waits for them, and re-layouts  8.54 us (4%)
    ppermute x14, waiting for transfers between devices, swap_chip(): lax.ppermute(v, 'row', [(i, i ^ 1 << orders[i & 1][step]) for i in range(...  50.8 us
    ppermute x7, waiting for transfers between devices, reach(): return lax.ppermute(v, 'col', [(i, i ^ distance) for i in range(n_col)])  23.9 us
    ppermute x7, starting transfers between devices, reach(): return lax.ppermute(v, 'col', [(i, i ^ distance) for i in range(n_col)])  19.8 us
    ppermute x14, starting transfers between devices, swap_chip(): lax.ppermute(v, 'row', [(i, i ^ 1 << orders[i & 1][step]) for i in range(...  17.7 us
    dot_general x4, matrix products, weight_grad(): lax.dot_general(piece, rows, (((0,), (0,)), ((), ())), preferred_element_...  17.1 us
    dot_general x4, matrix products, down(): return jnp.dot(flat(v), w, preferred_element_type=f32)  13 us
    dot_general x4, matrix products, up(): jnp.dot(v, w_in[:, h * cut:(h + 1) * cut], preferred_element_type=f32)  8.27 us
    ppermute x8, waiting for transfers between devices, swap_core(): return lax.ppermute(v, 'row', [(i, i ^ 1) for i in range(n_row)])  6.6 us
  transfers between devices with their start and end apart: 29, of which 16 were waited for; matrix products, arithmetic and copies ran while one was open for 29% of the time, Pallas kernels for 0%

profile of v1, /device:TPU:0, one launch (start us, length us, event | category | flops | bytes accessed | tf_op | source)
XLA Modules:
  0.0 197.2 jit_solution(14490272398124681070)
XLA Ops:
  2.9 3.1 %collective-permute-start = (bf16[2,2,1,32,1536]{4,3,2,1,0:T(8,128)(2,1)S(1)}, bf16[2,2,1,32,1536]{4,3,2,1,0:T(8,128)(2,1)S(1)}, u32[]{:S(2)}, u32[]{:S(2)}) collective-permute-start(bf16[2,2,1,32,1536]{4,3,2,1,0:T(8,128)(2,1)S(1)} %pad_maximum_fusion.10), channel_id=1, source_target_pairs={{0,1},{1,0},{2,3},{3,2},{4,5},{5,4},{6,7},{7,6},{8,9},{9,8},{10,11... | collective-permute-start | bytes 1179656 | tf_op jit(solution)/shard_map/ppermute | solution.py:119
  6.0 9.1 %collective-permute-done = bf16[2,2,1,32,1536]{4,3,2,1,0:T(8,128)(2,1)S(1)} collective-permute-done((bf16[2,2,1,32,1536]{4,3,2,1,0:T(8,128)(2,1)S(1)}, bf16[2,2,1,32,1536]{4,3,2,1,0:T(8,128)(2,1)S(1)}, u32[]{:S(2)}, u32[]{:S(2)}) %collective-permute-start) | collective-permute-done | bytes 393248 | tf_op jit(solution)/shard_map/ppermute | solution.py:119
  15.3 3.9 %fusion.16 = bf16[256,3072]{1,0:T(8,128)(2,1)S(1)} fusion(bf16[256,768]{1,0:T(8,128)(2,1)S(1)} %bitcast.125, bf16[768,6144]{1,0:T(8,128)(2,1)} %param.5), kind=kOutput, calls=%fused_computation.16 | convolution fusion | flops 1208745984 | bytes 6684672 | tf_op jit(solution)/shard_map/dot_general | solution.py:92
  26.1 3.4 %collective-permute-done.3 = bf16[256,3072]{1,0:T(8,128)(2,1)S(1)} collective-permute-done((bf16[256,3072]{1,0:T(8,128)(2,1)S(1)}, bf16[256,3072]{1,0:T(8,128)(2,1)S(1)}, u32[]{:S(2)}, u32[]{:S(2)}) %collective-permute-start.3) | collective-permute-done | bytes 1572896 | tf_op jit(solution)/shard_map/ppermute | solution.py:40
  37.5 4.9 %collective-permute-done.2 = bf16[128,3072]{1,0:T(8,128)(2,1)S(1)} collective-permute-done((bf16[128,3072]{1,0:T(8,128)(2,1)S(1)}, bf16[128,3072]{1,0:T(8,128)(2,1)S(1)}, u32[]{:S(2)}, u32[]{:S(2)}) %collective-permute-start.2) | collective-permute-done | bytes 786464 | tf_op jit(solution)/shard_map/ppermute | solution.py:43
  42.4 8.0 %collective-permute-done.5 = bf16[2,2,1,32,768]{4,3,2,1,0:T(8,128)(2,1)S(1)} collective-permute-done((bf16[2,2,1,32,768]{4,3,2,1,0:T(8,128)(2,1)S(1)}, bf16[2,2,1,32,768]{4,3,2,1,0:T(8,128)(2,1)S(1)}, u32[]{:S(2)}, u32[]{:S(2)}) %collective-permute-start.5) | collective-permute-done | bytes 196640 | tf_op jit(solution)/shard_map/ppermute | solution.py:119
  54.1 3.2 %collective-permute-done.8 = bf16[256,3072]{1,0:T(8,128)(2,1)S(1)} collective-permute-done((bf16[256,3072]{1,0:T(8,128)(2,1)S(1)}, bf16[256,3072]{1,0:T(8,128)(2,1)S(1)}, u32[]{:S(2)}, u32[]{:S(2)}) %collective-permute-start.8) | collective-permute-done | bytes 1572896 | tf_op jit(solution)/shard_map/ppermute | solution.py:40
  60.1 5.1 %collective-permute-start.11 = (bf16[2,2,1,32,768]{4,3,2,1,0:T(8,128)(2,1)S(1)}, bf16[2,2,1,32,768]{4,3,2,1,0:T(8,128)(2,1)S(1)}, u32[]{:S(2)}, u32[]{:S(2)}) collective-permute-start(bf16[2,2,1,32,768]{4,3,2,1,0:T(8,128)(2,1)S(1)} %reverse_select_fusion.2), channel_id=1, source_target_pairs={{0,2},{1,3},{2,0},{3,1},{4,6},{5,7},{6,4},{7,5},{8,10},{9,11},{10,... | collective-permute-start | bytes 589832 | tf_op jit(solution)/shard_map/ppermute | solution.py:119
  69.0 4.7 %collective-permute-done.4 = bf16[64,3072]{1,0:T(8,128)(2,1)S(1)} collective-permute-done((bf16[64,3072]{1,0:T(8,128)(2,1)S(1)}, bf16[64,3072]{1,0:T(8,128)(2,1)S(1)}, u32[]{:S(2)}, u32[]{:S(2)}) %collective-permute-start.4) | collective-permute-done | bytes 393248 | tf_op jit(solution)/shard_map/ppermute | solution.py:43
  73.6 4.2 %collective-permute-done.12 = bf16[64,3072]{1,0:T(8,128)(2,1)S(1)} collective-permute-done((bf16[64,3072]{1,0:T(8,128)(2,1)S(1)}, bf16[64,3072]{1,0:T(8,128)(2,1)S(1)}, u32[]{:S(2)}, u32[]{:S(2)}) %collective-permute-start.12) | collective-permute-done | bytes 393248 | tf_op jit(solution)/shard_map/ppermute | solution.py:43
  85.1 5.2 %collective-permute-done.13 = bf16[64,3072]{1,0:T(8,128)(2,1)S(1)} collective-permute-done((bf16[64,3072]{1,0:T(8,128)(2,1)S(1)}, bf16[64,3072]{1,0:T(8,128)(2,1)S(1)}, u32[]{:S(2)}, u32[]{:S(2)}) %collective-permute-start.13) | collective-permute-done | bytes 393248 | tf_op jit(solution)/shard_map/ppermute | solution.py:43
  94.5 17.1 %collective-permute-done.16 = bf16[128,3072]{1,0:T(8,128)(2,1)S(1)} collective-permute-done((bf16[128,3072]{1,0:T(8,128)(2,1)S(1)}, bf16[128,3072]{1,0:T(8,128)(2,1)S(1)}, u32[]{:S(2)}, u32[]{:S(2)}) %collective-permute-start.16) | collective-permute-done | bytes 786464 | tf_op jit(solution)/shard_map/ppermute | solution.py:43
  114.8 9.2 %collective-permute-done.18 = bf16[64,3072]{1,0:T(8,128)(2,1)S(1)} collective-permute-done((bf16[64,3072]{1,0:T(8,128)(2,1)S(1)}, bf16[64,3072]{1,0:T(8,128)(2,1)S(1)}, u32[]{:S(2)}, u32[]{:S(2)}) %collective-permute-start.18) | collective-permute-done | bytes 393248 | tf_op jit(solution)/shard_map/ppermute | solution.py:43
  127.5 4.2 %collective-permute-done.17 = bf16[1,2,4,32,1536]{4,3,2,1,0:T(8,128)(2,1)} collective-permute-done((bf16[1,2,4,32,1536]{4,3,2,1,0:T(8,128)(2,1)S(1)}, bf16[1,2,4,32,1536]{4,3,2,1,0:T(8,128)(2,1)}, u32[]{:S(2)}, u32[]{:S(2)}) %collective-permute-start.17) | collective-permute-done | bytes 786464 | tf_op jit(solution)/shard_map/ppermute | solution.py:43
  134.2 4.4 %broadcast_in_dim.6 = bf16[6144,768]{1,0:T(8,128)(2,1)} broadcast(bf16[]{:T(256)} %constant.30.clone.1), dimensions={} | broadcast | bytes 9437186 | tf_op jit(solution)/shard_map/broadcast_in_dim | solution.py:187
  138.5 4.2 %fusion.47 = bf16[6144,768]{1,0:T(8,128)(2,1)} fusion(bf16[6144,768]{1,0:T(8,128)(2,1)} %broadcast_in_dim.6, s32[]{:T(128)S(6)} %select_n.161, bf16[512,1536]{1,0:T(8,128)(2,1)} %bitcast.24, bf16[512,768]{1,0:T(8,128)(2,1)S(1)} %bitcast.118), kind=kOutput, calls=%fused_computation.39 | convolution fusion | flops 1209139200 | bytes 4718596 | tf_op jit(solution)/shard_map/dot_general | solution.py:28
  149.3 3.5 %fusion.52 = f32[512,768]{1,0:T(8,128)S(1)} fusion(bf16[512,1536]{1,0:T(8,128)(2,1)} %bitcast.27, bf16[6144,768]{1,0:T(8,128)(2,1)} %param.6, s32[]{:T(128)S(6)} %select_n.162), kind=kOutput, calls=%fused_computation.49 | convolution fusion | flops 1207959552 | bytes 5505028 | tf_op jit(solution)/shard_map/dot_general | solution.py:183
  152.9 3.7 %fusion.63 = f32[512,768]{1,0:T(8,128)S(1)} fusion(f32[512,768]{1,0:T(8,128)S(1)} %fusion.52, bf16[512,1536]{1,0:T(8,128)(2,1)} %bitcast.24, bf16[6144,768]{1,0:T(8,128)(2,1)} %param.6, s32[]{:T(128)S(6)} %select_n.161), kind=kOutput, calls=%fused_computation.80 | convolution fusion | flops 1208352768 | bytes 7077892 | tf_op jit(solution)/shard_map/dot_general | solution.py:183
  156.6 4.4 %fusion.46 = bf16[6144,768]{1,0:T(8,128)(2,1)} fusion(bf16[6144,768]{1,0:T(8,128)(2,1)} %fusion.47, s32[]{:T(128)S(6)} %select_n.163, bf16[512,1536]{1,0:T(8,128)(2,1)} %bitcast.28, bf16[512,768]{1,0:T(8,128)(2,1)S(1)} %bitcast.116), kind=kOutput, calls=%fused_computation.37 | convolution fusion | flops 1209139200 | bytes 4718596 | tf_op jit(solution)/shard_map/dot_general | solution.py:28
  161.0 3.0 %fusion.48 = f32[512,768]{1,0:T(8,128)S(1)} fusion(bf16[512,1536]{1,0:T(8,128)(2,1)} %bitcast.29, bf16[6144,768]{1,0:T(8,128)(2,1)S(1)} %bitcast.123, s32[]{:T(128)S(6)} %select_n.164), kind=kOutput, calls=%fused_computation.45 | convolution fusion | flops 1207959552 | bytes 5505028 | tf_op jit(solution)/shard_map/dot_general | solution.py:183
  167.2 4.0 %collective-permute-start.23 = (bf16[2,2,2,32,768]{4,3,1,0,2:T(8,128)(2,1)S(1)}, bf16[2,2,2,32,768]{4,3,1,0,2:T(8,128)(2,1)S(1)}, u32[]{:S(2)}, u32[]{:S(2)}) collective-permute-start(bf16[2,2,2,32,768]{4,3,1,0,2:T(8,128)(2,1)S(1)} %bitcast.126), channel_id=1, source_target_pairs={{0,1},{1,0},{2,3},{3,2},{4,5},{5,4},{6,7},{7,6},{8,9},{9,8},{10,11... | collective-permute-start | bytes 1179656 | tf_op jit(solution)/shard_map/ppermute | solution.py:119
  171.2 4.2 %fusion.45 = bf16[6144,768]{1,0:T(8,128)(2,1)} fusion(bf16[6144,768]{1,0:T(8,128)(2,1)} %fusion.46, s32[]{:T(128)S(6)} %select_n.162, bf16[512,1536]{1,0:T(8,128)(2,1)} %bitcast.27, bf16[512,768]{1,0:T(8,128)(2,1)S(1)} %bitcast.119), kind=kOutput, calls=%fused_computation.35 | convolution fusion | flops 1209139200 | bytes 4718596 | tf_op jit(solution)/shard_map/dot_general | solution.py:28
  175.5 4.2 %fusion.44 = bf16[6144,768]{1,0:T(8,128)(2,1)} fusion(bf16[6144,768]{1,0:T(8,128)(2,1)} %fusion.45, s32[]{:T(128)S(6)} %select_n.164, bf16[512,1536]{1,0:T(8,128)(2,1)} %bitcast.29, bf16[512,768]{1,0:T(8,128)(2,1)S(1)} %bitcast.117), kind=kOutput, calls=%fused_computation.33 | convolution fusion | flops 1209139200 | bytes 4718596 | tf_op jit(solution)/shard_map/dot_general | solution.py:28
  191.4 5.0 %collective-permute-done.25 = bf16[2,2,1,32,768]{4,3,2,1,0:T(8,128)(2,1)S(1)} collective-permute-done((bf16[2,2,1,32,768]{4,3,2,1,0:T(8,128)(2,1)S(1)}, bf16[2,2,1,32,768]{4,3,2,1,0:T(8,128)(2,1)S(1)}, u32[]{:S(2)}, u32[]{:S(2)}) %collective-permute-start.25) | collective-permute-done | bytes 196640 | tf_op jit(solution)/shard_map/ppermute | solution.py:119
  (135 shorter events, 69.9 us)
Async XLA Ops:
  2.9 12.2 %collective-permute-start = (bf16[2,2,1,32,1536]{4,3,2,1,0:T(8,128)(2,1)S(1)}, bf16[2,2,1,32,1536]{4,3,2,1,0:T(8,128)(2,1)S(1)}, u32[]{:S(2)}, u32[]{:S(2)}) collective-permute-start(bf16[2,2,1,32,1536]{4,3,2,1,0:T(8,128)(2,1)S(1)} %pad_maximum_fusion.10), channel_id=1, source_target_pairs={{0,1},{1,0},{2,3},{3,2},{4,5},{5,4},{6,7},{7,6},{8,9},{9,8},{10,11... | collective-permute-start | bytes 1179656 | tf_op jit(solution)/shard_map/ppermute | solution.py:119
  30.4 12.1 %collective-permute-start.2 = (bf16[128,3072]{1,0:T(8,128)(2,1)S(1)}, bf16[128,3072]{1,0:T(8,128)(2,1)S(1)}, u32[]{:S(2)}, u32[]{:S(2)}) collective-permute-start(bf16[128,3072]{1,0:T(8,128)(2,1)S(1)} %slice.126), channel_id=1, source_target_pairs={{0,8},{4,20},{8,0},{12,28},{16,24},{20,4},{24,16},{28,12},{1,9},{5... | collective-permute-start | bytes 2359304 | tf_op jit(solution)/shard_map/ppermute | solution.py:43
  33.0 17.9 %collective-permute-start.7 = (bf16[128,3072]{1,0:T(8,128)(2,1)S(1)}, bf16[128,3072]{1,0:T(8,128)(2,1)S(1)}, u32[]{:S(2)}, u32[]{:S(2)}) collective-permute-start(bf16[128,3072]{1,0:T(8,128)(2,1)S(1)} %slice.130), channel_id=1, source_target_pairs={{0,8},{4,20},{8,0},{12,28},{16,24},{20,4},{24,16},{28,12},{1,9},{5... | collective-permute-start | bytes 2359304 | tf_op jit(solution)/shard_map/ppermute | solution.py:43
  33.4 17.0 %collective-permute-start.5 = (bf16[2,2,1,32,768]{4,3,2,1,0:T(8,128)(2,1)S(1)}, bf16[2,2,1,32,768]{4,3,2,1,0:T(8,128)(2,1)S(1)}, u32[]{:S(2)}, u32[]{:S(2)}) collective-permute-start(bf16[2,2,1,32,768]{4,3,2,1,0:T(8,128)(2,1)S(1)} %reverse_select_fusion.4), channel_id=1, source_target_pairs={{0,2},{1,3},{2,0},{3,1},{4,6},{5,7},{6,4},{7,5},{8,10},{9,11},{10,... | collective-permute-start | bytes 589832 | tf_op jit(solution)/shard_map/ppermute | solution.py:119
  36.1 14.3 %collective-permute-start.6 = (bf16[2,2,1,32,768]{4,3,2,1,0:T(8,128)(2,1)S(1)}, bf16[2,2,1,32,768]{4,3,2,1,0:T(8,128)(2,1)S(1)}, u32[]{:S(2)}, u32[]{:S(2)}) collective-permute-start(bf16[2,2,1,32,768]{4,3,2,1,0:T(8,128)(2,1)S(1)} %reverse_select_fusion.4), channel_id=1, source_target_pairs={{0,3},{1,2},{2,1},{3,0},{4,7},{5,6},{6,5},{7,4},{8,11},{9,10},{10,... | collective-permute-start | bytes 589832 | tf_op jit(solution)/shard_map/ppermute | solution.py:119
  58.2 20.7 %collective-permute-start.9 = (bf16[128,3072]{1,0:T(8,128)(2,1)S(1)}, bf16[128,3072]{1,0:T(8,128)(2,1)S(1)}, u32[]{:S(2)}, u32[]{:S(2)}) collective-permute-start(bf16[128,3072]{1,0:T(8,128)(2,1)S(1)} %slice.132), channel_id=1, source_target_pairs={{0,8},{4,20},{8,0},{12,28},{16,24},{20,4},{24,16},{28,12},{1,9},{5... | collective-permute-start | bytes 2359304 | tf_op jit(solution)/shard_map/ppermute | solution.py:43
  60.1 18.8 %collective-permute-start.11 = (bf16[2,2,1,32,768]{4,3,2,1,0:T(8,128)(2,1)S(1)}, bf16[2,2,1,32,768]{4,3,2,1,0:T(8,128)(2,1)S(1)}, u32[]{:S(2)}, u32[]{:S(2)}) collective-permute-start(bf16[2,2,1,32,768]{4,3,2,1,0:T(8,128)(2,1)S(1)} %reverse_select_fusion.2), channel_id=1, source_target_pairs={{0,2},{1,3},{2,0},{3,1},{4,6},{5,7},{6,4},{7,5},{8,10},{9,11},{10,... | collective-permute-start | bytes 589832 | tf_op jit(solution)/shard_map/ppermute | solution.py:119
  65.2 13.6 %collective-permute-start.10 = (bf16[2,2,1,32,768]{4,3,2,1,0:T(8,128)(2,1)S(1)}, bf16[2,2,1,32,768]{4,3,2,1,0:T(8,128)(2,1)S(1)}, u32[]{:S(2)}, u32[]{:S(2)}) collective-permute-start(bf16[2,2,1,32,768]{4,3,2,1,0:T(8,128)(2,1)S(1)} %reverse_select_fusion.2), channel_id=1, source_target_pairs={{0,3},{1,2},{2,1},{3,0},{4,7},{5,6},{6,5},{7,4},{8,11},{9,10},{10,... | collective-permute-start | bytes 589832 | tf_op jit(solution)/shard_map/ppermute | solution.py:119
  65.7 7.9 %collective-permute-start.4 = (bf16[64,3072]{1,0:T(8,128)(2,1)S(1)}, bf16[64,3072]{1,0:T(8,128)(2,1)S(1)}, u32[]{:S(2)}, u32[]{:S(2)}) collective-permute-start(bf16[64,3072]{1,0:T(8,128)(2,1)S(1)} %slice.129), channel_id=1, source_target_pairs={{0,16},{4,12},{8,24},{12,4},{16,0},{20,28},{24,8},{28,20},{1,17},{... | collective-permute-start | bytes 1179656 | tf_op jit(solution)/shard_map/ppermute | solution.py:43
  67.3 10.5 %collective-permute-start.12 = (bf16[64,3072]{1,0:T(8,128)(2,1)S(1)}, bf16[64,3072]{1,0:T(8,128)(2,1)S(1)}, u32[]{:S(2)}, u32[]{:S(2)}) collective-permute-start(bf16[64,3072]{1,0:T(8,128)(2,1)S(1)} %slice.134), channel_id=1, source_target_pairs={{0,16},{4,12},{8,24},{12,4},{16,0},{20,28},{24,8},{28,20},{1,17},{... | collective-permute-start | bytes 1179656 | tf_op jit(solution)/shard_map/ppermute | solution.py:43
  82.0 8.2 %collective-permute-start.15 = (bf16[256,3072]{1,0:T(8,128)(2,1)S(1)}, bf16[256,3072]{1,0:T(8,128)(2,1)S(1)}, u32[]{:S(2)}, u32[]{:S(2)}) collective-permute-start(bf16[256,3072]{1,0:T(8,128)(2,1)S(1)} %get-tuple-element.97), channel_id=1, source_target_pairs={{0,4},{4,0},{8,12},{12,8},{16,20},{20,16},{24,28},{28,24},{1,5},{5... | collective-permute-start | bytes 4718600 | tf_op jit(solution)/shard_map/ppermute | solution.py:40
  82.4 7.8 %collective-permute-start.13 = (bf16[64,3072]{1,0:T(8,128)(2,1)S(1)}, bf16[64,3072]{1,0:T(8,128)(2,1)S(1)}, u32[]{:S(2)}, u32[]{:S(2)}) collective-permute-start(bf16[64,3072]{1,0:T(8,128)(2,1)S(1)} %slice.136), channel_id=1, source_target_pairs={{0,16},{4,12},{8,24},{12,4},{16,0},{20,28},{24,8},{28,20},{1,17},{... | collective-permute-start | bytes 1179656 | tf_op jit(solution)/shard_map/ppermute | solution.py:43
  91.1 20.5 %collective-permute-start.16 = (bf16[128,3072]{1,0:T(8,128)(2,1)S(1)}, bf16[128,3072]{1,0:T(8,128)(2,1)S(1)}, u32[]{:S(2)}, u32[]{:S(2)}) collective-permute-start(bf16[128,3072]{1,0:T(8,128)(2,1)S(1)} %slice.137), channel_id=1, source_target_pairs={{0,8},{4,20},{8,0},{12,28},{16,24},{20,4},{24,16},{28,12},{1,9},{5... | collective-permute-start | bytes 2359304 | tf_op jit(solution)/shard_map/ppermute | solution.py:43
  92.9 20.3 %collective-permute-start.14 = (bf16[1,1,4,32,3072]{4,3,2,1,0:T(8,128)(2,1)S(1)}, bf16[1,1,4,32,3072]{4,3,2,1,0:T(8,128)(2,1)S(1)}, u32[]{:S(2)}, u32[]{:S(2)}) collective-permute-start(bf16[1,1,4,32,3072]{4,3,2,1,0:T(8,128)(2,1)S(1)} %get-tuple-element.78), channel_id=1, source_target_pairs={{0,16},{4,12},{8,24},{12,4},{16,0},{20,28},{24,8},{28,20},{1,17},{... | collective-permute-start | bytes 2359304 | tf_op jit(solution)/shard_map/ppermute | solution.py:43
  111.8 12.1 %collective-permute-start.18 = (bf16[64,3072]{1,0:T(8,128)(2,1)S(1)}, bf16[64,3072]{1,0:T(8,128)(2,1)S(1)}, u32[]{:S(2)}, u32[]{:S(2)}) collective-permute-start(bf16[64,3072]{1,0:T(8,128)(2,1)S(1)} %slice.141), channel_id=1, source_target_pairs={{0,16},{4,12},{8,24},{12,4},{16,0},{20,28},{24,8},{28,20},{1,17},{... | collective-permute-start | bytes 1179656 | tf_op jit(solution)/shard_map/ppermute | solution.py:43
  113.4 18.3 %collective-permute-start.17 = (bf16[1,2,4,32,1536]{4,3,2,1,0:T(8,128)(2,1)S(1)}, bf16[1,2,4,32,1536]{4,3,2,1,0:T(8,128)(2,1)}, u32[]{:S(2)}, u32[]{:S(2)}) collective-permute-start(bf16[1,2,4,32,1536]{4,3,2,1,0:T(8,128)(2,1)S(1)} %get-tuple-element.75), channel_id=1, source_target_pairs={{0,8},{4,20},{8,0},{12,28},{16,24},{20,4},{24,16},{28,12},{1,9},{5... | collective-permute-start | bytes 2359304 | tf_op jit(solution)/shard_map/ppermute | solution.py:43
  124.8 18.7 %collective-permute-start.20 = (bf16[1,1,4,32,3072]{4,3,2,1,0:T(8,128)(2,1)S(1)}, bf16[1,1,4,32,3072]{4,3,2,1,0:T(8,128)(2,1)}, u32[]{:S(2)}, u32[]{:S(2)}) collective-permute-start(bf16[1,1,4,32,3072]{4,3,2,1,0:T(8,128)(2,1)S(1)} %fusion.61), channel_id=1, source_target_pairs={{0,16},{4,12},{8,24},{12,4},{16,0},{20,28},{24,8},{28,20},{1,17},{... | collective-permute-start | bytes 2359304 | tf_op jit(solution)/shard_map/ppermute | solution.py:43
  126.1 17.5 %collective-permute-start.19 = (bf16[1,2,4,32,1536]{4,3,2,1,0:T(8,128)(2,1)S(1)}, bf16[1,2,4,32,1536]{4,3,2,1,0:T(8,128)(2,1)}, u32[]{:S(2)}, u32[]{:S(2)}) collective-permute-start(bf16[1,2,4,32,1536]{4,3,2,1,0:T(8,128)(2,1)S(1)} %get-tuple-element.76), channel_id=1, source_target_pairs={{0,8},{4,20},{8,0},{12,28},{16,24},{20,4},{24,16},{28,12},{1,9},{5... | collective-permute-start | bytes 2359304 | tf_op jit(solution)/shard_map/ppermute | solution.py:43
  134.1 22.4 %collective-permute-start.21 = (bf16[2,2,4,32,1536]{4,3,2,1,0:T(8,128)(2,1)}, bf16[2,2,4,32,1536]{4,3,2,1,0:T(8,128)(2,1)}, u32[]{:S(2)}, u32[]{:S(2)}) collective-permute-start(bf16[2,2,4,32,1536]{4,3,2,1,0:T(8,128)(2,1)} %pad_maximum_fusion.1), channel_id=1, source_target_pairs={{0,4},{4,0},{8,12},{12,8},{16,20},{20,16},{24,28},{28,24},{1,5},{5... | collective-permute-start | bytes 4718600 | tf_op jit(solution)/shard_map/ppermute | solution.py:40
  146.0 15.0 %collective-permute-start.22 = (bf16[2,2,4,32,1536]{4,3,2,1,0:T(8,128)(2,1)}, bf16[2,2,4,32,1536]{4,3,2,1,0:T(8,128)(2,1)}, u32[]{:S(2)}, u32[]{:S(2)}) collective-permute-start(bf16[2,2,4,32,1536]{4,3,2,1,0:T(8,128)(2,1)} %pad_maximum_fusion.3), channel_id=1, source_target_pairs={{0,4},{4,0},{8,12},{12,8},{16,20},{20,16},{24,28},{28,24},{1,5},{5... | collective-permute-start | bytes 4718600 | tf_op jit(solution)/shard_map/ppermute | solution.py:40
  147.2 32.5 %collective-permute-start.24 = (bf16[1,2,4,32,1536]{4,3,2,1,0:T(8,128)(2,1)S(1)}, bf16[1,2,4,32,1536]{4,3,2,1,0:T(8,128)(2,1)S(1)}, u32[]{:S(2)}, u32[]{:S(2)}) collective-permute-start(bf16[1,2,4,32,1536]{4,3,2,1,0:T(8,128)(2,1)S(1)} %get-tuple-element.74), channel_id=1, source_target_pairs={{0,8},{4,20},{8,0},{12,28},{16,24},{20,4},{24,16},{28,12},{1,9},{5... | collective-permute-start | bytes 2359304 | tf_op jit(solution)/shard_map/ppermute | solution.py:43
  149.0 34.4 %collective-permute-start.26 = (bf16[1,2,4,32,1536]{4,3,2,1,0:T(8,128)(2,1)S(1)}, bf16[1,2,4,32,1536]{4,3,2,1,0:T(8,128)(2,1)S(1)}, u32[]{:S(2)}, u32[]{:S(2)}) collective-permute-start(bf16[1,2,4,32,1536]{4,3,2,1,0:T(8,128)(2,1)S(1)} %get-tuple-element.73), channel_id=1, source_target_pairs={{0,8},{4,20},{8,0},{12,28},{16,24},{20,4},{24,16},{28,12},{1,9},{5... | collective-permute-start | bytes 2359304 | tf_op jit(solution)/shard_map/ppermute | solution.py:43
  167.2 13.2 %collective-permute-start.23 = (bf16[2,2,2,32,768]{4,3,1,0,2:T(8,128)(2,1)S(1)}, bf16[2,2,2,32,768]{4,3,1,0,2:T(8,128)(2,1)S(1)}, u32[]{:S(2)}, u32[]{:S(2)}) collective-permute-start(bf16[2,2,2,32,768]{4,3,1,0,2:T(8,128)(2,1)S(1)} %bitcast.126), channel_id=1, source_target_pairs={{0,1},{1,0},{2,3},{3,2},{4,5},{5,4},{6,7},{7,6},{8,9},{9,8},{10,11... | collective-permute-start | bytes 1179656 | tf_op jit(solution)/shard_map/ppermute | solution.py:119
  184.1 12.3 %collective-permute-start.25 = (bf16[2,2,1,32,768]{4,3,2,1,0:T(8,128)(2,1)S(1)}, bf16[2,2,1,32,768]{4,3,2,1,0:T(8,128)(2,1)S(1)}, u32[]{:S(2)}, u32[]{:S(2)}) collective-permute-start(bf16[2,2,1,32,768]{4,3,2,1,0:T(8,128)(2,1)S(1)} %slice_bitcast_fusion), channel_id=1, source_target_pairs={{0,2},{1,3},{2,0},{3,1},{4,6},{5,7},{6,4},{7,5},{8,10},{9,11},{10,... | collective-permute-start | bytes 589832 | tf_op jit(solution)/shard_map/ppermute | solution.py:119
  (16 other events, 80.4 us)

commit v2 on v1

--- a/solution.py
+++ b/solution.py
@@ -184,8 +184,7 @@
 
         own = [doubled(acts[0], 0)]
         got = [swap_core(own[0])]
-        grad_w_out = weight_grad(flat(own[0]), c_rows[0], own_half, 0, jnp.zeros_like(w_out), False)
-        grad = quarters(lax.concatenate([grad[0], take(grad[1], grad_w_out)], 1))
+        grad = quarters(doubled(grad, 1))
         grads = [(v, swap_chip(v, 0)) for v in grad]
         own.append(doubled(acts[1], 0))
         got.append(swap_core(own[1]))
@@ -208,21 +207,20 @@
         def merged(flight, *also):
             return (flight[0].astype(f32) + take(flight[1], *also).astype(f32)).astype(bf16)
 
-        for half, rows, v, p in (
-            (other_half, c_rows[1], got[0], 0),
-            (own_half, c_rows[0], own[1], 1),
-            (other_half, c_rows[1], got[1], 1),
-        ):
-            grad_w_out = weight_grad(flat(v), rows, half, p, grad_w_out, False)
-        grads[0] = grads[0][0], take(grads[0][1], mixed, grad_w_out)
+        grads[0] = grads[0][0], take(grads[0][1], mixed)
         mixed = halve(mixed, 0)
-        mixed = merged(mixed)
+        grad_w_out = jnp.zeros_like(w_out)
+        own = [after(v, got[1]) for v in own]
+        for p in range(2):
+            for i, (half, v) in enumerate(((own_half, own), (other_half, got))):
+                grad_w_out = weight_grad(flat(v[p]), c_rows[i], half, p, grad_w_out, False)
+        mixed = merged(mixed, grad_w_out)
         grads[0] = lax.concatenate([grads[0][0], after(grads[0][1], mixed)], 0)
         grads[0] = grads[0], swap_core(grads[0])
         grad_w_in = weight_grad(flat(grads[0][0]), x_rows[0], own_half, 0, jnp.zeros_like(w_in), True)
         for bit in range(1, col_bits):
             mixed = halve(mixed if bit == 1 else merged(mixed), bit)
-        grads[1] = lax.concatenate([grads[1][0], take(grads[1][1], grad_w_in)], 0)
+        grads[1] = lax.concatenate([grads[1][0], take(grads[1][1])], 0)
         grads[1] = grads[1], swap_core(grads[1])
         grads[0] = grads[0][0], take(grads[0][1])
         for p, i in ((0, 1), (1, 0)):

time: 198 us -> 199 us (level)
  waiting for transfers between devices: 81.2 us -> 85.9 us
    ppermute x14, waiting for transfers between devices: 50.8 us -> 61.2 us  [swap_chip(): lax.ppermute(v, 'row', [(i, i ^ 1 << orders[i & 1][step]) for i in range(...]
    dot_general x4, matrix products: 17.1 us -> 10.2 us  [weight_grad(): lax.dot_general(piece, rows, (((0,), (0,)), ((), ())), preferred_element_...]
    dot_general x4, matrix products: 5.67 us -> 11.7 us  [weight_grad(): out = jnp.dot(rows, piece, preferred_element_type=f32).astype(bf16)]
    ppermute x7, waiting for transfers between devices: 23.9 us -> 18.1 us  [reach(): return lax.ppermute(v, 'col', [(i, i ^ distance) for i in range(n_col)])]
    broadcast_in_dim x1, local copies, waits for them, and re-layouts: 4.35 us -> 0.61 us  [per_device(): grad_w_out = jnp.zeros_like(w_out)]
    concatenate x3 -> x4, other arithmetic: 5.02 us -> 1.75 us  [doubled(): return lax.concatenate([flight[0], take(flight[1])], k)]
    unnamed x24 -> x32, local copies, waits for them, and re-layouts: 2.49 us -> 4.59 us
  transfers between devices with their start and end apart: 29 -> 29, of which waited for: 16 -> 14; matrix products, arithmetic and copies ran while one was open for 29% -> 26% of each run, Pallas kernels for 0% -> 0%
where the time goes in v2:
time: 199 us; the launch traced here: 198 us
  waiting for transfers between devices  85.9 us (43%)
  matrix products  48.5 us (24%)
  starting transfers between devices  36.5 us (18%)
  other arithmetic  18.6 us (9%)
  local copies, waits for them, and re-layouts  7.57 us (4%)
    ppermute x14, waiting for transfers between devices, swap_chip(): lax.ppermute(v, 'row', [(i, i ^ 1 << orders[i & 1][step]) for i in range(...  61.2 us
    ppermute x7, waiting for transfers between devices, reach(): return lax.ppermute(v, 'col', [(i, i ^ distance) for i in range(n_col)])  18.1 us
    ppermute x7, starting transfers between devices, reach(): return lax.ppermute(v, 'col', [(i, i ^ distance) for i in range(n_col)])  18 us
    ppermute x14, starting transfers between devices, swap_chip(): lax.ppermute(v, 'row', [(i, i ^ 1 << orders[i & 1][step]) for i in range(...  17.7 us
    dot_general x4, matrix products, down(): return jnp.dot(flat(v), w, preferred_element_type=f32)  12.5 us
    dot_general x4, matrix products, weight_grad(): out = jnp.dot(rows, piece, preferred_element_type=f32).astype(bf16)  11.7 us
    dot_general x4, matrix products, weight_grad(): lax.dot_general(piece, rows, (((0,), (0,)), ((), ())), preferred_element_...  10.2 us
    dot_general x4, matrix products, up(): jnp.dot(v, w_in[:, h * cut:(h + 1) * cut], preferred_element_type=f32)  8.32 us
  transfers between devices with their start and end apart: 29, of which 14 were waited for; matrix products, arithmetic and copies ran while one was open for 26% of the time, Pallas kernels for 0%

profile of v2, /device:TPU:0, one launch (start us, length us, event | category | flops | bytes accessed | tf_op | source)
XLA Modules:
  0.0 198.5 jit_solution(12320445194368497569)
XLA Ops:
  2.9 3.1 %collective-permute-start = (bf16[2,2,1,32,1536]{4,3,2,1,0:T(8,128)(2,1)S(1)}, bf16[2,2,1,32,1536]{4,3,2,1,0:T(8,128)(2,1)S(1)}, u32[]{:S(2)}, u32[]{:S(2)}) collective-permute-start(bf16[2,2,1,32,1536]{4,3,2,1,0:T(8,128)(2,1)S(1)} %pad_maximum_fusion.10), channel_id=1, source_target_pairs={{0,1},{1,0},{2,3},{3,2},{4,5},{5,4},{6,7},{7,6},{8,9},{9,8},{10,11... | collective-permute-start | bytes 1179656 | tf_op jit(solution)/shard_map/ppermute | solution.py:119
  6.0 9.1 %collective-permute-done = bf16[2,2,1,32,1536]{4,3,2,1,0:T(8,128)(2,1)S(1)} collective-permute-done((bf16[2,2,1,32,1536]{4,3,2,1,0:T(8,128)(2,1)S(1)}, bf16[2,2,1,32,1536]{4,3,2,1,0:T(8,128)(2,1)S(1)}, u32[]{:S(2)}, u32[]{:S(2)}) %collective-permute-start) | collective-permute-done | bytes 393248 | tf_op jit(solution)/shard_map/ppermute | solution.py:119
  15.3 3.9 %fusion.16 = bf16[256,3072]{1,0:T(8,128)(2,1)S(1)} fusion(bf16[256,768]{1,0:T(8,128)(2,1)S(1)} %bitcast.127, bf16[768,6144]{1,0:T(8,128)(2,1)} %param.5), kind=kOutput, calls=%fused_computation.16 | convolution fusion | flops 1208745984 | bytes 6684672 | tf_op jit(solution)/shard_map/dot_general | solution.py:92
  26.1 3.4 %collective-permute-done.3 = bf16[256,3072]{1,0:T(8,128)(2,1)S(1)} collective-permute-done((bf16[256,3072]{1,0:T(8,128)(2,1)S(1)}, bf16[256,3072]{1,0:T(8,128)(2,1)S(1)}, u32[]{:S(2)}, u32[]{:S(2)}) %collective-permute-start.3) | collective-permute-done | bytes 1572896 | tf_op jit(solution)/shard_map/ppermute | solution.py:40
  37.5 4.9 %collective-permute-done.2 = bf16[128,3072]{1,0:T(8,128)(2,1)S(1)} collective-permute-done((bf16[128,3072]{1,0:T(8,128)(2,1)S(1)}, bf16[128,3072]{1,0:T(8,128)(2,1)S(1)}, u32[]{:S(2)}, u32[]{:S(2)}) %collective-permute-start.2) | collective-permute-done | bytes 786464 | tf_op jit(solution)/shard_map/ppermute | solution.py:43
  42.4 8.0 %collective-permute-done.5 = bf16[2,2,1,32,768]{4,3,2,1,0:T(8,128)(2,1)S(1)} collective-permute-done((bf16[2,2,1,32,768]{4,3,2,1,0:T(8,128)(2,1)S(1)}, bf16[2,2,1,32,768]{4,3,2,1,0:T(8,128)(2,1)S(1)}, u32[]{:S(2)}, u32[]{:S(2)}) %collective-permute-start.5) | collective-permute-done | bytes 196640 | tf_op jit(solution)/shard_map/ppermute | solution.py:119
  54.1 3.2 %collective-permute-done.8 = bf16[256,3072]{1,0:T(8,128)(2,1)S(1)} collective-permute-done((bf16[256,3072]{1,0:T(8,128)(2,1)S(1)}, bf16[256,3072]{1,0:T(8,128)(2,1)S(1)}, u32[]{:S(2)}, u32[]{:S(2)}) %collective-permute-start.8) | collective-permute-done | bytes 1572896 | tf_op jit(solution)/shard_map/ppermute | solution.py:40
  60.1 5.1 %collective-permute-start.11 = (bf16[2,2,1,32,768]{4,3,2,1,0:T(8,128)(2,1)S(1)}, bf16[2,2,1,32,768]{4,3,2,1,0:T(8,128)(2,1)S(1)}, u32[]{:S(2)}, u32[]{:S(2)}) collective-permute-start(bf16[2,2,1,32,768]{4,3,2,1,0:T(8,128)(2,1)S(1)} %reverse_select_fusion.2), channel_id=1, source_target_pairs={{0,2},{1,3},{2,0},{3,1},{4,6},{5,7},{6,4},{7,5},{8,10},{9,11},{10,... | collective-permute-start | bytes 589832 | tf_op jit(solution)/shard_map/ppermute | solution.py:119
  69.2 4.4 %collective-permute-done.4 = bf16[64,3072]{1,0:T(8,128)(2,1)S(1)} collective-permute-done((bf16[64,3072]{1,0:T(8,128)(2,1)S(1)}, bf16[64,3072]{1,0:T(8,128)(2,1)S(1)}, u32[]{:S(2)}, u32[]{:S(2)}) %collective-permute-start.4) | collective-permute-done | bytes 393248 | tf_op jit(solution)/shard_map/ppermute | solution.py:43
  73.6 4.2 %collective-permute-done.12 = bf16[64,3072]{1,0:T(8,128)(2,1)S(1)} collective-permute-done((bf16[64,3072]{1,0:T(8,128)(2,1)S(1)}, bf16[64,3072]{1,0:T(8,128)(2,1)S(1)}, u32[]{:S(2)}, u32[]{:S(2)}) %collective-permute-start.12) | collective-permute-done | bytes 393248 | tf_op jit(solution)/shard_map/ppermute | solution.py:43
  85.1 5.1 %collective-permute-done.13 = bf16[64,3072]{1,0:T(8,128)(2,1)S(1)} collective-permute-done((bf16[64,3072]{1,0:T(8,128)(2,1)S(1)}, bf16[64,3072]{1,0:T(8,128)(2,1)S(1)}, u32[]{:S(2)}, u32[]{:S(2)}) %collective-permute-start.13) | collective-permute-done | bytes 393248 | tf_op jit(solution)/shard_map/ppermute | solution.py:43
  94.4 17.1 %collective-permute-done.16 = bf16[128,3072]{1,0:T(8,128)(2,1)S(1)} collective-permute-done((bf16[128,3072]{1,0:T(8,128)(2,1)S(1)}, bf16[128,3072]{1,0:T(8,128)(2,1)S(1)}, u32[]{:S(2)}, u32[]{:S(2)}) %collective-permute-start.16) | collective-permute-done | bytes 786464 | tf_op jit(solution)/shard_map/ppermute | solution.py:43
  114.8 9.1 %collective-permute-done.18 = bf16[64,3072]{1,0:T(8,128)(2,1)S(1)} collective-permute-done((bf16[64,3072]{1,0:T(8,128)(2,1)S(1)}, bf16[64,3072]{1,0:T(8,128)(2,1)S(1)}, u32[]{:S(2)}, u32[]{:S(2)}) %collective-permute-start.18) | collective-permute-done | bytes 393248 | tf_op jit(solution)/shard_map/ppermute | solution.py:43
  127.4 4.4 %collective-permute-done.17 = bf16[1,2,4,32,1536]{4,3,2,1,0:T(8,128)(2,1)S(1)} collective-permute-done((bf16[1,2,4,32,1536]{4,3,2,1,0:T(8,128)(2,1)S(1)}, bf16[1,2,4,32,1536]{4,3,2,1,0:T(8,128)(2,1)S(1)}, u32[]{:S(2)}, u32[]{:S(2)}) %collective-permute-start.17) | collective-permute-done | bytes 786464 | tf_op jit(solution)/shard_map/ppermute | solution.py:43
  132.1 11.3 %collective-permute-done.20 = bf16[1,1,4,32,3072]{4,3,2,1,0:T(8,128)(2,1)S(1)} collective-permute-done((bf16[1,1,4,32,3072]{4,3,2,1,0:T(8,128)(2,1)S(1)}, bf16[1,1,4,32,3072]{4,3,2,1,0:T(8,128)(2,1)S(1)}, u32[]{:S(2)}, u32[]{:S(2)}) %collective-permute-start.20) | collective-permute-done | bytes 786464 | tf_op jit(solution)/shard_map/ppermute | solution.py:43
  147.0 3.7 %fusion.52 = f32[512,768]{1,0:T(8,128)S(1)} fusion(bf16[512,1536]{1,0:T(8,128)(2,1)} %bitcast.27, bf16[6144,768]{1,0:T(8,128)(2,1)} %param.6, s32[]{:T(128)S(6)} %select_n.162), kind=kOutput, calls=%fused_computation.49 | convolution fusion | flops 1207959552 | bytes 5505028 | tf_op jit(solution)/shard_map/dot_general | solution.py:183
  150.7 3.1 %fusion.63 = f32[512,768]{1,0:T(8,128)S(1)} fusion(f32[512,768]{1,0:T(8,128)S(1)} %fusion.52, bf16[512,1536]{1,0:T(8,128)(2,1)S(1)} %bitcast.110, bf16[6144,768]{1,0:T(8,128)(2,1)} %param.6, s32[]{:T(128)S(6)} %select_n.161), kind=kOutput, calls=%fused_computation.80 | convolution fusion | flops 1208352768 | bytes 7077892 | tf_op jit(solution)/shard_map/dot_general | solution.py:183
  156.7 2.9 %broadcast_select_fusion.4 = (f32[512,768]{1,0:T(8,128)S(1)}, f32[512,768]{1,0:T(8,128)S(1)}) fusion(f32[512,768]{1,0:T(8,128)S(1)} %fusion.63, pred[]{:T(512)S(6)} %eq.8, f32[512,768]{1,0:T(8,128)S(1)} %fusion.48, bf16[512,1536]{1,0:T(8,128)(2,1)} %bitcast.28, bf16[6144,768]{1,0:T(8,128)(2,1)S(1)} %bitcast.125, s32[]{:T(128)S(6)} %select_n.163), kind=kOutput, calls=%fused_computation.98 | convolution fusion | flops 1209139200 | bytes 10223621 | tf_op jit(solution)/shard_map/dot_general | solution.py:183
  159.9 4.0 %collective-permute-start.23 = (bf16[2,2,2,32,768]{4,3,1,0,2:T(8,128)(2,1)S(1)}, bf16[2,2,2,32,768]{4,3,1,0,2:T(8,128)(2,1)S(1)}, u32[]{:S(2)}, u32[]{:S(2)}) collective-permute-start(bf16[2,2,2,32,768]{4,3,1,0,2:T(8,128)(2,1)S(1)} %bitcast.128), channel_id=1, source_target_pairs={{0,1},{1,0},{2,3},{3,2},{4,5},{5,4},{6,7},{7,6},{8,9},{9,8},{10,11... | collective-permute-start | bytes 1179656 | tf_op jit(solution)/shard_map/ppermute | solution.py:119
  167.2 2.8 %fusion.46 = bf16[6144,768]{1,0:T(8,128)(2,1)S(1)} fusion(bf16[6144,768]{1,0:T(8,128)(2,1)S(1)} %fusion.47, s32[]{:T(128)S(6)} %select_n.163, bf16[512,1536]{1,0:T(8,128)(2,1)} %bitcast.28, bf16[512,768]{1,0:T(8,128)(2,1)S(1)} %bitcast.118), kind=kOutput, calls=%fused_computation.37 | convolution fusion | flops 1209139200 | bytes 4718596 | tf_op jit(solution)/shard_map/dot_general | solution.py:28
  170.1 2.8 %fusion.45 = bf16[6144,768]{1,0:T(8,128)(2,1)S(1)} fusion(bf16[6144,768]{1,0:T(8,128)(2,1)S(1)} %fusion.46, s32[]{:T(128)S(6)} %select_n.162, bf16[512,1536]{1,0:T(8,128)(2,1)} %bitcast.37, bf16[512,768]{1,0:T(8,128)(2,1)S(1)} %bitcast.121), kind=kOutput, calls=%fused_computation.35 | convolution fusion | flops 1209139200 | bytes 4718596 | tf_op jit(solution)/shard_map/dot_general | solution.py:28
  172.9 2.8 %fusion.44 = bf16[6144,768]{1,0:T(8,128)(2,1)S(1)} fusion(bf16[6144,768]{1,0:T(8,128)(2,1)S(1)} %fusion.45, s32[]{:T(128)S(6)} %select_n.164, bf16[512,1536]{1,0:T(8,128)(2,1)} %bitcast.29, bf16[512,768]{1,0:T(8,128)(2,1)S(1)} %bitcast.119), kind=kOutput, calls=%fused_computation.33 | convolution fusion | flops 1209139200 | bytes 4718596 | tf_op jit(solution)/shard_map/dot_general | solution.py:28
  182.9 3.1 %fusion.43 = bf16[768,6144]{1,0:T(8,128)(2,1)S(1)} fusion(bf16[768,6144]{1,0:T(8,128)(2,1)S(1)} %broadcast_in_dim.7, s32[]{:T(128)S(6)} %select_n.161, bf16[768,512]{0,1:T(8,128)(2,1)} %bitcast.116, bf16[512,1536]{1,0:T(8,128)(2,1)} %bitcast.42), kind=kOutput, calls=%fused_computation.31 | convolution fusion | flops 1209139200 | bytes 4718596 | tf_op jit(solution)/shard_map/dot_general | solution.py:26
  186.1 2.9 %fusion.42 = bf16[768,6144]{1,0:T(8,128)(2,1)S(1)} fusion(bf16[768,6144]{1,0:T(8,128)(2,1)S(1)} %fusion.43, s32[]{:T(128)S(6)} %select_n.163, bf16[768,512]{0,1:T(8,128)(2,1)S(1)} %bitcast.114, bf16[512,1536]{1,0:T(8,128)(2,1)} %bitcast.43), kind=kOutput, calls=%fused_computation.29 | convolution fusion | flops 1209139200 | bytes 4718596 | tf_op jit(solution)/shard_map/dot_general | solution.py:26
  (143 shorter events, 72.3 us)
Async XLA Ops:
  2.9 12.2 %collective-permute-start = (bf16[2,2,1,32,1536]{4,3,2,1,0:T(8,128)(2,1)S(1)}, bf16[2,2,1,32,1536]{4,3,2,1,0:T(8,128)(2,1)S(1)}, u32[]{:S(2)}, u32[]{:S(2)}) collective-permute-start(bf16[2,2,1,32,1536]{4,3,2,1,0:T(8,128)(2,1)S(1)} %pad_maximum_fusion.10), channel_id=1, source_target_pairs={{0,1},{1,0},{2,3},{3,2},{4,5},{5,4},{6,7},{7,6},{8,9},{9,8},{10,11... | collective-permute-start | bytes 1179656 | tf_op jit(solution)/shard_map/ppermute | solution.py:119
  30.4 12.1 %collective-permute-start.2 = (bf16[128,3072]{1,0:T(8,128)(2,1)S(1)}, bf16[128,3072]{1,0:T(8,128)(2,1)S(1)}, u32[]{:S(2)}, u32[]{:S(2)}) collective-permute-start(bf16[128,3072]{1,0:T(8,128)(2,1)S(1)} %slice.126), channel_id=1, source_target_pairs={{0,8},{4,20},{8,0},{12,28},{16,24},{20,4},{24,16},{28,12},{1,9},{5... | collective-permute-start | bytes 2359304 | tf_op jit(solution)/shard_map/ppermute | solution.py:43
  33.0 17.9 %collective-permute-start.7 = (bf16[128,3072]{1,0:T(8,128)(2,1)S(1)}, bf16[128,3072]{1,0:T(8,128)(2,1)S(1)}, u32[]{:S(2)}, u32[]{:S(2)}) collective-permute-start(bf16[128,3072]{1,0:T(8,128)(2,1)S(1)} %slice.130), channel_id=1, source_target_pairs={{0,8},{4,20},{8,0},{12,28},{16,24},{20,4},{24,16},{28,12},{1,9},{5... | collective-permute-start | bytes 2359304 | tf_op jit(solution)/shard_map/ppermute | solution.py:43
  33.4 17.0 %collective-permute-start.5 = (bf16[2,2,1,32,768]{4,3,2,1,0:T(8,128)(2,1)S(1)}, bf16[2,2,1,32,768]{4,3,2,1,0:T(8,128)(2,1)S(1)}, u32[]{:S(2)}, u32[]{:S(2)}) collective-permute-start(bf16[2,2,1,32,768]{4,3,2,1,0:T(8,128)(2,1)S(1)} %reverse_select_fusion.4), channel_id=1, source_target_pairs={{0,2},{1,3},{2,0},{3,1},{4,6},{5,7},{6,4},{7,5},{8,10},{9,11},{10,... | collective-permute-start | bytes 589832 | tf_op jit(solution)/shard_map/ppermute | solution.py:119
  36.1 14.3 %collective-permute-start.6 = (bf16[2,2,1,32,768]{4,3,2,1,0:T(8,128)(2,1)S(1)}, bf16[2,2,1,32,768]{4,3,2,1,0:T(8,128)(2,1)S(1)}, u32[]{:S(2)}, u32[]{:S(2)}) collective-permute-start(bf16[2,2,1,32,768]{4,3,2,1,0:T(8,128)(2,1)S(1)} %reverse_select_fusion.4), channel_id=1, source_target_pairs={{0,3},{1,2},{2,1},{3,0},{4,7},{5,6},{6,5},{7,4},{8,11},{9,10},{10,... | collective-permute-start | bytes 589832 | tf_op jit(solution)/shard_map/ppermute | solution.py:119
  58.2 20.7 %collective-permute-start.9 = (bf16[128,3072]{1,0:T(8,128)(2,1)S(1)}, bf16[128,3072]{1,0:T(8,128)(2,1)S(1)}, u32[]{:S(2)}, u32[]{:S(2)}) collective-permute-start(bf16[128,3072]{1,0:T(8,128)(2,1)S(1)} %slice.132), channel_id=1, source_target_pairs={{0,8},{4,20},{8,0},{12,28},{16,24},{20,4},{24,16},{28,12},{1,9},{5... | collective-permute-start | bytes 2359304 | tf_op jit(solution)/shard_map/ppermute | solution.py:43
  60.1 18.8 %collective-permute-start.11 = (bf16[2,2,1,32,768]{4,3,2,1,0:T(8,128)(2,1)S(1)}, bf16[2,2,1,32,768]{4,3,2,1,0:T(8,128)(2,1)S(1)}, u32[]{:S(2)}, u32[]{:S(2)}) collective-permute-start(bf16[2,2,1,32,768]{4,3,2,1,0:T(8,128)(2,1)S(1)} %reverse_select_fusion.2), channel_id=1, source_target_pairs={{0,2},{1,3},{2,0},{3,1},{4,6},{5,7},{6,4},{7,5},{8,10},{9,11},{10,... | collective-permute-start | bytes 589832 | tf_op jit(solution)/shard_map/ppermute | solution.py:119
  65.2 13.6 %collective-permute-start.10 = (bf16[2,2,1,32,768]{4,3,2,1,0:T(8,128)(2,1)S(1)}, bf16[2,2,1,32,768]{4,3,2,1,0:T(8,128)(2,1)S(1)}, u32[]{:S(2)}, u32[]{:S(2)}) collective-permute-start(bf16[2,2,1,32,768]{4,3,2,1,0:T(8,128)(2,1)S(1)} %reverse_select_fusion.2), channel_id=1, source_target_pairs={{0,3},{1,2},{2,1},{3,0},{4,7},{5,6},{6,5},{7,4},{8,11},{9,10},{10,... | collective-permute-start | bytes 589832 | tf_op jit(solution)/shard_map/ppermute | solution.py:119
  65.7 7.9 %collective-permute-start.4 = (bf16[64,3072]{1,0:T(8,128)(2,1)S(1)}, bf16[64,3072]{1,0:T(8,128)(2,1)S(1)}, u32[]{:S(2)}, u32[]{:S(2)}) collective-permute-start(bf16[64,3072]{1,0:T(8,128)(2,1)S(1)} %slice.129), channel_id=1, source_target_pairs={{0,16},{4,12},{8,24},{12,4},{16,0},{20,28},{24,8},{28,20},{1,17},{... | collective-permute-start | bytes 1179656 | tf_op jit(solution)/shard_map/ppermute | solution.py:43
  67.3 10.5 %collective-permute-start.12 = (bf16[64,3072]{1,0:T(8,128)(2,1)S(1)}, bf16[64,3072]{1,0:T(8,128)(2,1)S(1)}, u32[]{:S(2)}, u32[]{:S(2)}) collective-permute-start(bf16[64,3072]{1,0:T(8,128)(2,1)S(1)} %slice.134), channel_id=1, source_target_pairs={{0,16},{4,12},{8,24},{12,4},{16,0},{20,28},{24,8},{28,20},{1,17},{... | collective-permute-start | bytes 1179656 | tf_op jit(solution)/shard_map/ppermute | solution.py:43
  82.0 8.2 %collective-permute-start.15 = (bf16[256,3072]{1,0:T(8,128)(2,1)S(1)}, bf16[256,3072]{1,0:T(8,128)(2,1)S(1)}, u32[]{:S(2)}, u32[]{:S(2)}) collective-permute-start(bf16[256,3072]{1,0:T(8,128)(2,1)S(1)} %get-tuple-element.101), channel_id=1, source_target_pairs={{0,4},{4,0},{8,12},{12,8},{16,20},{20,16},{24,28},{28,24},{1,5},{5... | collective-permute-start | bytes 4718600 | tf_op jit(solution)/shard_map/ppermute | solution.py:40
  91.1 20.5 %collective-permute-start.16 = (bf16[128,3072]{1,0:T(8,128)(2,1)S(1)}, bf16[128,3072]{1,0:T(8,128)(2,1)S(1)}, u32[]{:S(2)}, u32[]{:S(2)}) collective-permute-start(bf16[128,3072]{1,0:T(8,128)(2,1)S(1)} %slice.137), channel_id=1, source_target_pairs={{0,8},{4,20},{8,0},{12,28},{16,24},{20,4},{24,16},{28,12},{1,9},{5... | collective-permute-start | bytes 2359304 | tf_op jit(solution)/shard_map/ppermute | solution.py:43
  92.8 20.3 %collective-permute-start.14 = (bf16[1,1,4,32,3072]{4,3,2,1,0:T(8,128)(2,1)S(1)}, bf16[1,1,4,32,3072]{4,3,2,1,0:T(8,128)(2,1)S(1)}, u32[]{:S(2)}, u32[]{:S(2)}) collective-permute-start(bf16[1,1,4,32,3072]{4,3,2,1,0:T(8,128)(2,1)S(1)} %get-tuple-element.82), channel_id=1, source_target_pairs={{0,16},{4,12},{8,24},{12,4},{16,0},{20,28},{24,8},{28,20},{1,17},{... | collective-permute-start | bytes 2359304 | tf_op jit(solution)/shard_map/ppermute | solution.py:43
  111.8 12.1 %collective-permute-start.18 = (bf16[64,3072]{1,0:T(8,128)(2,1)S(1)}, bf16[64,3072]{1,0:T(8,128)(2,1)S(1)}, u32[]{:S(2)}, u32[]{:S(2)}) collective-permute-start(bf16[64,3072]{1,0:T(8,128)(2,1)S(1)} %slice.141), channel_id=1, source_target_pairs={{0,16},{4,12},{8,24},{12,4},{16,0},{20,28},{24,8},{28,20},{1,17},{... | collective-permute-start | bytes 1179656 | tf_op jit(solution)/shard_map/ppermute | solution.py:43
  113.3 18.5 %collective-permute-start.17 = (bf16[1,2,4,32,1536]{4,3,2,1,0:T(8,128)(2,1)S(1)}, bf16[1,2,4,32,1536]{4,3,2,1,0:T(8,128)(2,1)S(1)}, u32[]{:S(2)}, u32[]{:S(2)}) collective-permute-start(bf16[1,2,4,32,1536]{4,3,2,1,0:T(8,128)(2,1)S(1)} %get-tuple-element.79), channel_id=1, source_target_pairs={{0,8},{4,20},{8,0},{12,28},{16,24},{20,4},{24,16},{28,12},{1,9},{5... | collective-permute-start | bytes 2359304 | tf_op jit(solution)/shard_map/ppermute | solution.py:43
  124.7 18.7 %collective-permute-start.20 = (bf16[1,1,4,32,3072]{4,3,2,1,0:T(8,128)(2,1)S(1)}, bf16[1,1,4,32,3072]{4,3,2,1,0:T(8,128)(2,1)S(1)}, u32[]{:S(2)}, u32[]{:S(2)}) collective-permute-start(bf16[1,1,4,32,3072]{4,3,2,1,0:T(8,128)(2,1)S(1)} %fusion.61), channel_id=1, source_target_pairs={{0,16},{4,12},{8,24},{12,4},{16,0},{20,28},{24,8},{28,20},{1,17},{... | collective-permute-start | bytes 2359304 | tf_op jit(solution)/shard_map/ppermute | solution.py:43
  126.0 17.4 %collective-permute-start.19 = (bf16[1,2,4,32,1536]{4,3,2,1,0:T(8,128)(2,1)S(1)}, bf16[1,2,4,32,1536]{4,3,2,1,0:T(8,128)(2,1)S(1)}, u32[]{:S(2)}, u32[]{:S(2)}) collective-permute-start(bf16[1,2,4,32,1536]{4,3,2,1,0:T(8,128)(2,1)S(1)} %get-tuple-element.80), channel_id=1, source_target_pairs={{0,8},{4,20},{8,0},{12,28},{16,24},{20,4},{24,16},{28,12},{1,9},{5... | collective-permute-start | bytes 2359304 | tf_op jit(solution)/shard_map/ppermute | solution.py:43
  132.0 21.8 %collective-permute-start.21 = (bf16[2,2,4,32,1536]{4,3,2,1,0:T(8,128)(2,1)S(1)}, bf16[2,2,4,32,1536]{4,3,2,1,0:T(8,128)(2,1)}, u32[]{:S(2)}, u32[]{:S(2)}) collective-permute-start(bf16[2,2,4,32,1536]{4,3,2,1,0:T(8,128)(2,1)S(1)} %pad_maximum_fusion.1), channel_id=1, source_target_pairs={{0,4},{4,0},{8,12},{12,8},{16,20},{20,16},{24,28},{28,24},{1,5},{5... | collective-permute-start | bytes 4718600 | tf_op jit(solution)/shard_map/ppermute | solution.py:40
  144.7 9.1 %collective-permute-start.22 = (bf16[2,2,4,32,1536]{4,3,2,1,0:T(8,128)(2,1)}, bf16[2,2,4,32,1536]{4,3,2,1,0:T(8,128)(2,1)}, u32[]{:S(2)}, u32[]{:S(2)}) collective-permute-start(bf16[2,2,4,32,1536]{4,3,2,1,0:T(8,128)(2,1)} %pad_maximum_fusion.3), channel_id=1, source_target_pairs={{0,4},{4,0},{8,12},{12,8},{16,20},{20,16},{24,28},{28,24},{1,5},{5... | collective-permute-start | bytes 4718600 | tf_op jit(solution)/shard_map/ppermute | solution.py:40
  144.9 28.0 %collective-permute-start.24 = (bf16[1,2,4,32,1536]{4,3,2,1,0:T(8,128)(2,1)S(1)}, bf16[1,2,4,32,1536]{4,3,2,1,0:T(8,128)(2,1)S(1)}, u32[]{:S(2)}, u32[]{:S(2)}) collective-permute-start(bf16[1,2,4,32,1536]{4,3,2,1,0:T(8,128)(2,1)S(1)} %get-tuple-element.78), channel_id=1, source_target_pairs={{0,8},{4,20},{8,0},{12,28},{16,24},{20,4},{24,16},{28,12},{1,9},{5... | collective-permute-start | bytes 2359304 | tf_op jit(solution)/shard_map/ppermute | solution.py:43
  146.7 30.8 %collective-permute-start.26 = (bf16[1,2,4,32,1536]{4,3,2,1,0:T(8,128)(2,1)S(1)}, bf16[1,2,4,32,1536]{4,3,2,1,0:T(8,128)(2,1)S(1)}, u32[]{:S(2)}, u32[]{:S(2)}) collective-permute-start(bf16[1,2,4,32,1536]{4,3,2,1,0:T(8,128)(2,1)S(1)} %get-tuple-element.77), channel_id=1, source_target_pairs={{0,8},{4,20},{8,0},{12,28},{16,24},{20,4},{24,16},{28,12},{1,9},{5... | collective-permute-start | bytes 2359304 | tf_op jit(solution)/shard_map/ppermute | solution.py:43
  159.9 15.9 %collective-permute-start.23 = (bf16[2,2,2,32,768]{4,3,1,0,2:T(8,128)(2,1)S(1)}, bf16[2,2,2,32,768]{4,3,1,0,2:T(8,128)(2,1)S(1)}, u32[]{:S(2)}, u32[]{:S(2)}) collective-permute-start(bf16[2,2,2,32,768]{4,3,1,0,2:T(8,128)(2,1)S(1)} %bitcast.128), channel_id=1, source_target_pairs={{0,1},{1,0},{2,3},{3,2},{4,5},{5,4},{6,7},{7,6},{8,9},{9,8},{10,11... | collective-permute-start | bytes 1179656 | tf_op jit(solution)/shard_map/ppermute | solution.py:119
  177.4 8.6 %collective-permute-start.28 = (bf16[2,2,4,32,1536]{4,3,2,1,0:T(8,128)(2,1)}, bf16[2,2,4,32,1536]{4,3,2,1,0:T(8,128)(2,1)}, u32[]{:S(2)}, u32[]{:S(2)}) collective-permute-start(bf16[2,2,4,32,1536]{4,3,2,1,0:T(8,128)(2,1)} %pad_maximum_fusion.5), channel_id=1, source_target_pairs={{0,4},{4,0},{8,12},{12,8},{16,20},{20,16},{24,28},{28,24},{1,5},{5... | collective-permute-start | bytes 4718600 | tf_op jit(solution)/shard_map/ppermute | solution.py:40
  180.5 14.2 %collective-permute-start.25 = (bf16[2,2,1,32,768]{4,3,2,1,0:T(8,128)(2,1)}, bf16[2,2,1,32,768]{4,3,2,1,0:T(8,128)(2,1)}, u32[]{:S(2)}, u32[]{:S(2)}) collective-permute-start(bf16[2,2,1,32,768]{4,3,2,1,0:T(8,128)(2,1)} %slice_bitcast_fusion), channel_id=1, source_target_pairs={{0,2},{1,3},{2,0},{3,1},{4,6},{5,7},{6,4},{7,5},{8,10},{9,11},{10,... | collective-permute-start | bytes 589832 | tf_op jit(solution)/shard_map/ppermute | solution.py:119
  (20 other events, 105.2 us)

commit v3 on v2

--- a/solution.py
+++ b/solution.py
@@ -140,17 +140,14 @@
         x_rows = [lax.optimization_barrier(v.T) for v in ordered(x_all)]
         grad_near = steps_on(grad_near, 2, steps)
         grads = [total(grad_near[0], take(grad_near[1], *x_rows))]
+        hid_far = steps_on(hid_far, 1, steps)
+        hids.append(total(hid_far[0], take(hid_far[1])))
+        hid = lax.concatenate(hids, steps)
+        act = gelu_parts(hid)[0].astype(bf16)
         c_far = lax.concatenate([take(v) for v in c_far], steps)
-        hid_far = hid_far[0], take(hid_far[1])
-        c_far = after(c_far, hid_far[1])
         c_all = lax.concatenate([c_near, c_far], steps)
         c_rows = [lax.optimization_barrier(v) for v in ordered(c_all)]
         grad_far = back(c_far)
-        hid_far = step(*hid_far, 1)
-        hid_far = steps_on(hid_far, 2, steps)
-        hids.append(total(hid_far[0], take(hid_far[1])))
-        hid = lax.concatenate(hids, steps)
-        act = gelu_parts(hid)[0].astype(bf16)
 
         def doubled(flight, k):
             return lax.concatenate([flight[0], take(flight[1])], k)
@@ -168,27 +165,29 @@
             return [v[..., p * quarter : (p + 1) * quarter] for p in range(2)]
 
         act = chips(act, 1, steps)
-        grad_far = step(grad_far[0], take(grad_far[1]), 0)
-        grad_far = grad_far[0], take(grad_far[1], *c_rows)
         act = quarters(doubled(act, 1))
-        grad_far = step(*grad_far, 1)
         acts = [(v, swap_chip(v, 0)) for v in act]
+        grad_far = step(grad_far[0], take(grad_far[1], *c_rows), 0)
+        own = [doubled(acts[0], 0)]
+        got = [swap_core(own[0])]
+        grad_far = step(grad_far[0], take(grad_far[1]), 1)
+        own.append(doubled(acts[1], 0))
+        got.append(swap_core(own[1]))
         grad_far = steps_on(grad_far, 2, steps)
         grads.append(total(grad_far[0], take(grad_far[1])))
         grad = lax.concatenate(grads, steps)
         hid, grad = lax.optimization_barrier((hid, grad))
         grad = chips((grad * gelu_parts(hid)[1]).astype(bf16), 1, steps)
+        got[0] = take(got[0])
+        grad = grad[0], take(grad[1])
+        late = grad[1]
+        grad = quarters(lax.concatenate(grad, 1))
+        grads = [(v, swap_chip(v, 0)) for v in grad]
+        got[1] = take(got[1])
         def down(v, half, p):
             w = lax.dynamic_slice_in_dim(w_out, (half * 2 + p) * quarter, quarter, 0)
             return jnp.dot(flat(v), w, preferred_element_type=f32)
 
-        own = [doubled(acts[0], 0)]
-        got = [swap_core(own[0])]
-        grad = quarters(doubled(grad, 1))
-        grads = [(v, swap_chip(v, 0)) for v in grad]
-        own.append(doubled(acts[1], 0))
-        got.append(swap_core(own[1]))
-        got = [take(v) for v in got]
         sums = [
             (down(v[0], half, 0) + down(v[1], half, 1)).reshape(x_all.shape)
             for v, half in ((own, own_half), (got, other_half))
@@ -210,7 +209,7 @@
         grads[0] = grads[0][0], take(grads[0][1], mixed)
         mixed = halve(mixed, 0)
         grad_w_out = jnp.zeros_like(w_out)
-        own = [after(v, got[1]) for v in own]
+        own = [after(v, late) for v in own]
         for p in range(2):
             for i, (half, v) in enumerate(((own_half, own), (other_half, got))):
                 grad_w_out = weight_grad(flat(v[p]), c_rows[i], half, p, grad_w_out, False)

time: 199 us -> 199 us (level)
  matrix products: 48.5 us -> 43.4 us
  other arithmetic: 18.6 us -> 22.5 us
  local copies, waits for them, and re-layouts: 7.57 us -> 11 us
    ppermute x8, waiting for transfers between devices: 6.6 us -> 3.4 us  [swap_core(): return lax.ppermute(v, 'row', [(i, i ^ 1) for i in range(n_row)])]
    dot_general x4, matrix products: 10.2 us -> 7.11 us  [weight_grad(): lax.dot_general(piece, rows, (((0,), (0,)), ((), ())), preferred_element_...]
    unnamed x32 -> x41, local copies, waits for them, and re-layouts: 4.59 us -> 7.14 us
    ppermute x7, starting transfers between devices: 18 us -> 15.6 us  [reach(): return lax.ppermute(v, 'col', [(i, i ^ distance) for i in range(n_col)])]
    ppermute x7, waiting for transfers between devices: 18.1 us -> 20.5 us  [reach(): return lax.ppermute(v, 'col', [(i, i ^ distance) for i in range(n_col)])]
  transfers between devices with their start and end apart: 29 -> 29, of which waited for: 14 -> 14; matrix products, arithmetic and copies ran while one was open for 26% -> 27% of each run, Pallas kernels for 0% -> 0%
where the time goes in v3:
time: 199 us; the launch traced here: 198 us
  waiting for transfers between devices  84.8 us (43%)
  matrix products  43.4 us (22%)
  starting transfers between devices  35.4 us (18%)
  other arithmetic  22.5 us (11%)
  local copies, waits for them, and re-layouts  11 us (6%)
    ppermute x14, waiting for transfers between devices, swap_chip(): lax.ppermute(v, 'row', [(i, i ^ 1 << orders[i & 1][step]) for i in range(...  60.8 us
    ppermute x7, waiting for transfers between devices, reach(): return lax.ppermute(v, 'col', [(i, i ^ distance) for i in range(n_col)])  20.5 us
    ppermute x14, starting transfers between devices, swap_chip(): lax.ppermute(v, 'row', [(i, i ^ 1 << orders[i & 1][step]) for i in range(...  18.9 us
    ppermute x7, starting transfers between devices, reach(): return lax.ppermute(v, 'col', [(i, i ^ distance) for i in range(n_col)])  15.6 us
    dot_general x4, matrix products, weight_grad(): out = jnp.dot(rows, piece, preferred_element_type=f32).astype(bf16)  11.7 us
    dot_general x4, matrix products, down(): return jnp.dot(flat(v), w, preferred_element_type=f32)  10.5 us
    dot_general x4, matrix products, up(): jnp.dot(v, w_in[:, h * cut:(h + 1) * cut], preferred_element_type=f32)  8.19 us
    unnamed x41, local copies, waits for them, and re-layouts  7.14 us
  transfers between devices with their start and end apart: 29, of which 14 were waited for; matrix products, arithmetic and copies ran while one was open for 27% of the time, Pallas kernels for 0%

profile of v3, /device:TPU:0, one launch (start us, length us, event | category | flops | bytes accessed | tf_op | source)
XLA Modules:
  0.0 198.4 jit_solution(15647561605502020144)
XLA Ops:
  2.9 3.1 %collective-permute-start = (bf16[2,2,1,32,1536]{4,3,2,1,0:T(8,128)(2,1)S(1)}, bf16[2,2,1,32,1536]{4,3,2,1,0:T(8,128)(2,1)S(1)}, u32[]{:S(2)}, u32[]{:S(2)}) collective-permute-start(bf16[2,2,1,32,1536]{4,3,2,1,0:T(8,128)(2,1)S(1)} %pad_maximum_fusion.10), channel_id=1, source_target_pairs={{0,1},{1,0},{2,3},{3,2},{4,5},{5,4},{6,7},{7,6},{8,9},{9,8},{10,11... | collective-permute-start | bytes 1179656 | tf_op jit(solution)/shard_map/ppermute | solution.py:119
  6.0 9.1 %collective-permute-done = bf16[2,2,1,32,1536]{4,3,2,1,0:T(8,128)(2,1)S(1)} collective-permute-done((bf16[2,2,1,32,1536]{4,3,2,1,0:T(8,128)(2,1)S(1)}, bf16[2,2,1,32,1536]{4,3,2,1,0:T(8,128)(2,1)S(1)}, u32[]{:S(2)}, u32[]{:S(2)}) %collective-permute-start) | collective-permute-done | bytes 393248 | tf_op jit(solution)/shard_map/ppermute | solution.py:119
  15.3 3.9 %fusion.16 = bf16[256,3072]{1,0:T(8,128)(2,1)S(1)} fusion(bf16[256,768]{1,0:T(8,128)(2,1)S(1)} %bitcast.131, bf16[768,6144]{1,0:T(8,128)(2,1)} %param.5), kind=kOutput, calls=%fused_computation.16 | convolution fusion | flops 1208745984 | bytes 6684672 | tf_op jit(solution)/shard_map/dot_general | solution.py:92
  26.1 3.4 %collective-permute-done.3 = bf16[256,3072]{1,0:T(8,128)(2,1)S(1)} collective-permute-done((bf16[256,3072]{1,0:T(8,128)(2,1)S(1)}, bf16[256,3072]{1,0:T(8,128)(2,1)S(1)}, u32[]{:S(2)}, u32[]{:S(2)}) %collective-permute-start.3) | collective-permute-done | bytes 1572896 | tf_op jit(solution)/shard_map/ppermute | solution.py:40
  37.5 4.9 %collective-permute-done.2 = bf16[128,3072]{1,0:T(8,128)(2,1)S(1)} collective-permute-done((bf16[128,3072]{1,0:T(8,128)(2,1)S(1)}, bf16[128,3072]{1,0:T(8,128)(2,1)S(1)}, u32[]{:S(2)}, u32[]{:S(2)}) %collective-permute-start.2) | collective-permute-done | bytes 786464 | tf_op jit(solution)/shard_map/ppermute | solution.py:43
  42.4 8.0 %collective-permute-done.5 = bf16[2,2,1,32,768]{4,3,2,1,0:T(8,128)(2,1)S(1)} collective-permute-done((bf16[2,2,1,32,768]{4,3,2,1,0:T(8,128)(2,1)S(1)}, bf16[2,2,1,32,768]{4,3,2,1,0:T(8,128)(2,1)S(1)}, u32[]{:S(2)}, u32[]{:S(2)}) %collective-permute-start.5) | collective-permute-done | bytes 196640 | tf_op jit(solution)/shard_map/ppermute | solution.py:119
  53.9 5.3 %collective-permute-start.14 = (bf16[2,2,1,32,768]{4,3,2,1,0:T(8,128)(2,1)S(1)}, bf16[2,2,1,32,768]{4,3,2,1,0:T(8,128)(2,1)S(1)}, u32[]{:S(2)}, u32[]{:S(2)}) collective-permute-start(bf16[2,2,1,32,768]{4,3,2,1,0:T(8,128)(2,1)S(1)} %reverse_select_fusion.2), channel_id=1, source_target_pairs={{0,2},{1,3},{2,0},{3,1},{4,6},{5,7},{6,4},{7,5},{8,10},{9,11},{10,... | collective-permute-start | bytes 589832 | tf_op jit(solution)/shard_map/ppermute | solution.py:119
  66.0 4.8 %collective-permute-done.4 = bf16[64,3072]{1,0:T(8,128)(2,1)S(1)} collective-permute-done((bf16[64,3072]{1,0:T(8,128)(2,1)S(1)}, bf16[64,3072]{1,0:T(8,128)(2,1)S(1)}, u32[]{:S(2)}, u32[]{:S(2)}) %collective-permute-start.4) | collective-permute-done | bytes 393248 | tf_op jit(solution)/shard_map/ppermute | solution.py:43
  70.8 8.4 %collective-permute-done.10 = bf16[64,3072]{1,0:T(8,128)(2,1)S(1)} collective-permute-done((bf16[64,3072]{1,0:T(8,128)(2,1)S(1)}, bf16[64,3072]{1,0:T(8,128)(2,1)S(1)}, u32[]{:S(2)}, u32[]{:S(2)}) %collective-permute-start.10) | collective-permute-done | bytes 393248 | tf_op jit(solution)/shard_map/ppermute | solution.py:43
  81.9 6.2 %collective-permute-done.11 = bf16[64,3072]{1,0:T(8,128)(2,1)S(1)} collective-permute-done((bf16[64,3072]{1,0:T(8,128)(2,1)S(1)}, bf16[64,3072]{1,0:T(8,128)(2,1)S(1)}, u32[]{:S(2)}, u32[]{:S(2)}) %collective-permute-start.11) | collective-permute-done | bytes 393248 | tf_op jit(solution)/shard_map/ppermute | solution.py:43
  94.7 9.1 %collective-permute-done.12 = bf16[1,1,4,32,3072]{4,3,2,1,0:T(8,128)(2,1)S(1)} collective-permute-done((bf16[1,1,4,32,3072]{4,3,2,1,0:T(8,128)(2,1)S(1)}, bf16[1,1,4,32,3072]{4,3,2,1,0:T(8,128)(2,1)S(1)}, u32[]{:S(2)}, u32[]{:S(2)}) %collective-permute-start.12) | collective-permute-done | bytes 786464 | tf_op jit(solution)/shard_map/ppermute | solution.py:43
  111.4 6.5 %collective-permute-done.15 = bf16[1,2,4,32,1536]{4,3,2,1,0:T(8,128)(2,1)} collective-permute-done((bf16[1,2,4,32,1536]{4,3,2,1,0:T(8,128)(2,1)}, bf16[1,2,4,32,1536]{4,3,2,1,0:T(8,128)(2,1)}, u32[]{:S(2)}, u32[]{:S(2)}) %collective-permute-start.15) | collective-permute-done | bytes 786464 | tf_op jit(solution)/shard_map/ppermute | solution.py:43
  117.9 8.4 %collective-permute-done.18 = bf16[128,3072]{1,0:T(8,128)(2,1)} collective-permute-done((bf16[128,3072]{1,0:T(8,128)(2,1)}, bf16[128,3072]{1,0:T(8,128)(2,1)}, u32[]{:S(2)}, u32[]{:S(2)}) %collective-permute-start.18) | collective-permute-done | bytes 786464 | tf_op jit(solution)/shard_map/ppermute | solution.py:43
  130.9 7.9 %collective-permute-done.17 = bf16[1,2,4,32,1536]{4,3,2,1,0:T(8,128)(2,1)S(1)} collective-permute-done((bf16[1,2,4,32,1536]{4,3,2,1,0:T(8,128)(2,1)}, bf16[1,2,4,32,1536]{4,3,2,1,0:T(8,128)(2,1)S(1)}, u32[]{:S(2)}, u32[]{:S(2)}) %collective-permute-start.17) | collective-permute-done | bytes 786464 | tf_op jit(solution)/shard_map/ppermute | solution.py:43
  141.5 3.1 %fusion.52 = f32[512,768]{1,0:T(8,128)S(1)} fusion(bf16[512,1536]{1,0:T(8,128)(2,1)S(1)} %bitcast.108, bf16[6144,768]{1,0:T(8,128)(2,1)} %param.6, s32[]{:T(128)S(6)} %select_n.162), kind=kOutput, calls=%fused_computation.49 | convolution fusion | flops 1207959552 | bytes 5505028 | tf_op jit(solution)/shard_map/dot_general | solution.py:189
  144.6 3.1 %fusion.63 = f32[512,768]{1,0:T(8,128)S(1)} fusion(f32[512,768]{1,0:T(8,128)S(1)} %fusion.52, bf16[512,1536]{1,0:T(8,128)(2,1)S(1)} %bitcast.110, bf16[6144,768]{1,0:T(8,128)(2,1)} %param.6, s32[]{:T(128)S(6)} %select_n.160), kind=kOutput, calls=%fused_computation.80 | convolution fusion | flops 1208352768 | bytes 7077892 | tf_op jit(solution)/shard_map/dot_general | solution.py:189
  147.6 4.1 %collective-permute-done.22 = bf16[1,1,4,32,3072]{4,3,2,1,0:T(8,128)(2,1)S(1)} collective-permute-done((bf16[1,1,4,32,3072]{4,3,2,1,0:T(8,128)(2,1)S(1)}, bf16[1,1,4,32,3072]{4,3,2,1,0:T(8,128)(2,1)S(1)}, u32[]{:S(2)}, u32[]{:S(2)}) %collective-permute-start.22) | collective-permute-done | bytes 786464 | tf_op jit(solution)/shard_map/ppermute | solution.py:43
  159.4 3.0 %fusion.48 = f32[512,768]{1,0:T(8,128)S(1)} fusion(bf16[512,1536]{1,0:T(8,128)(2,1)} %bitcast.29, bf16[6144,768]{1,0:T(8,128)(2,1)S(1)} %bitcast.129, s32[]{:T(128)S(6)} %select_n.164), kind=kOutput, calls=%fused_computation.45 | convolution fusion | flops 1207959552 | bytes 5505028 | tf_op jit(solution)/shard_map/dot_general | solution.py:189
  166.6 2.8 %fusion.44 = bf16[6144,768]{1,0:T(8,128)(2,1)S(1)} fusion(bf16[6144,768]{1,0:T(8,128)(2,1)S(1)} %fusion.45, s32[]{:T(128)S(6)} %select_n.164, bf16[512,1536]{1,0:T(8,128)(2,1)} %bitcast.29, bf16[512,768]{1,0:T(8,128)(2,1)S(1)} %bitcast.123), kind=kOutput, calls=%fused_computation.33 | convolution fusion | flops 1209139200 | bytes 4718596 | tf_op jit(solution)/shard_map/dot_general | solution.py:28
  169.5 3.4 %collective-permute-done.23 = bf16[2,2,2,32,768]{4,3,1,0,2:T(8,128)(2,1)S(1)} collective-permute-done((bf16[2,2,2,32,768]{4,3,1,0,2:T(8,128)(2,1)S(1)}, bf16[2,2,2,32,768]{4,3,1,0,2:T(8,128)(2,1)S(1)}, u32[]{:S(2)}, u32[]{:S(2)}) %collective-permute-start.23) | collective-permute-done | bytes 393248 | tf_op jit(solution)/shard_map/ppermute | solution.py:119
  182.9 3.1 %fusion.43 = bf16[768,6144]{1,0:T(8,128)(2,1)S(1)} fusion(bf16[768,6144]{1,0:T(8,128)(2,1)S(1)} %broadcast_in_dim.7, s32[]{:T(128)S(6)} %select_n.160, bf16[768,512]{0,1:T(8,128)(2,1)} %bitcast.120, bf16[512,1536]{1,0:T(8,128)(2,1)} %bitcast.42), kind=kOutput, calls=%fused_computation.31 | convolution fusion | flops 1209139200 | bytes 4718596 | tf_op jit(solution)/shard_map/dot_general | solution.py:26
  186.0 2.9 %fusion.42 = bf16[768,6144]{1,0:T(8,128)(2,1)S(1)} fusion(bf16[768,6144]{1,0:T(8,128)(2,1)S(1)} %fusion.43, s32[]{:T(128)S(6)} %select_n.163, bf16[768,512]{0,1:T(8,128)(2,1)S(1)} %bitcast.118, bf16[512,1536]{1,0:T(8,128)(2,1)} %bitcast.43), kind=kOutput, calls=%fused_computation.29 | convolution fusion | flops 1209139200 | bytes 4718596 | tf_op jit(solution)/shard_map/dot_general | solution.py:26
  189.0 2.8 %fusion.41 = bf16[768,6144]{1,0:T(8,128)(2,1)S(1)} fusion(bf16[768,6144]{1,0:T(8,128)(2,1)S(1)} %fusion.42, s32[]{:T(128)S(6)} %select_n.162, bf16[768,512]{0,1:T(8,128)(2,1)S(1)} %bitcast.121, bf16[512,1536]{1,0:T(8,128)(2,1)} %bitcast.44), kind=kOutput, calls=%fused_computation.27 | convolution fusion | flops 1209139200 | bytes 4718596 | tf_op jit(solution)/shard_map/dot_general | solution.py:26
  191.8 2.8 %fusion.40 = bf16[768,6144]{1,0:T(8,128)(2,1)S(1)} fusion(bf16[768,6144]{1,0:T(8,128)(2,1)S(1)} %fusion.41, s32[]{:T(128)S(6)} %select_n.164, bf16[768,512]{0,1:T(8,128)(2,1)S(1)} %bitcast.119, bf16[512,1536]{1,0:T(8,128)(2,1)} %bitcast.45), kind=kOutput, calls=%fused_computation.25 | convolution fusion | flops 1209139200 | bytes 4718596 | tf_op jit(solution)/shard_map/dot_general | solution.py:26
  (152 shorter events, 76.8 us)
Async XLA Ops:
  2.9 12.2 %collective-permute-start = (bf16[2,2,1,32,1536]{4,3,2,1,0:T(8,128)(2,1)S(1)}, bf16[2,2,1,32,1536]{4,3,2,1,0:T(8,128)(2,1)S(1)}, u32[]{:S(2)}, u32[]{:S(2)}) collective-permute-start(bf16[2,2,1,32,1536]{4,3,2,1,0:T(8,128)(2,1)S(1)} %pad_maximum_fusion.10), channel_id=1, source_target_pairs={{0,1},{1,0},{2,3},{3,2},{4,5},{5,4},{6,7},{7,6},{8,9},{9,8},{10,11... | collective-permute-start | bytes 1179656 | tf_op jit(solution)/shard_map/ppermute | solution.py:119
  30.4 12.1 %collective-permute-start.2 = (bf16[128,3072]{1,0:T(8,128)(2,1)S(1)}, bf16[128,3072]{1,0:T(8,128)(2,1)S(1)}, u32[]{:S(2)}, u32[]{:S(2)}) collective-permute-start(bf16[128,3072]{1,0:T(8,128)(2,1)S(1)} %slice.126), channel_id=1, source_target_pairs={{0,8},{4,20},{8,0},{12,28},{16,24},{20,4},{24,16},{28,12},{1,9},{5... | collective-permute-start | bytes 2359304 | tf_op jit(solution)/shard_map/ppermute | solution.py:43
  33.0 17.9 %collective-permute-start.7 = (bf16[128,3072]{1,0:T(8,128)(2,1)S(1)}, bf16[128,3072]{1,0:T(8,128)(2,1)S(1)}, u32[]{:S(2)}, u32[]{:S(2)}) collective-permute-start(bf16[128,3072]{1,0:T(8,128)(2,1)S(1)} %slice.130), channel_id=1, source_target_pairs={{0,8},{4,20},{8,0},{12,28},{16,24},{20,4},{24,16},{28,12},{1,9},{5... | collective-permute-start | bytes 2359304 | tf_op jit(solution)/shard_map/ppermute | solution.py:43
  33.4 17.0 %collective-permute-start.5 = (bf16[2,2,1,32,768]{4,3,2,1,0:T(8,128)(2,1)S(1)}, bf16[2,2,1,32,768]{4,3,2,1,0:T(8,128)(2,1)S(1)}, u32[]{:S(2)}, u32[]{:S(2)}) collective-permute-start(bf16[2,2,1,32,768]{4,3,2,1,0:T(8,128)(2,1)S(1)} %reverse_select_fusion.4), channel_id=1, source_target_pairs={{0,2},{1,3},{2,0},{3,1},{4,6},{5,7},{6,4},{7,5},{8,10},{9,11},{10,... | collective-permute-start | bytes 589832 | tf_op jit(solution)/shard_map/ppermute | solution.py:119
  36.1 14.3 %collective-permute-start.6 = (bf16[2,2,1,32,768]{4,3,2,1,0:T(8,128)(2,1)S(1)}, bf16[2,2,1,32,768]{4,3,2,1,0:T(8,128)(2,1)S(1)}, u32[]{:S(2)}, u32[]{:S(2)}) collective-permute-start(bf16[2,2,1,32,768]{4,3,2,1,0:T(8,128)(2,1)S(1)} %reverse_select_fusion.4), channel_id=1, source_target_pairs={{0,3},{1,2},{2,1},{3,0},{4,7},{5,6},{6,5},{7,4},{8,11},{9,10},{10,... | collective-permute-start | bytes 589832 | tf_op jit(solution)/shard_map/ppermute | solution.py:119
  53.9 34.2 %collective-permute-start.14 = (bf16[2,2,1,32,768]{4,3,2,1,0:T(8,128)(2,1)S(1)}, bf16[2,2,1,32,768]{4,3,2,1,0:T(8,128)(2,1)S(1)}, u32[]{:S(2)}, u32[]{:S(2)}) collective-permute-start(bf16[2,2,1,32,768]{4,3,2,1,0:T(8,128)(2,1)S(1)} %reverse_select_fusion.2), channel_id=1, source_target_pairs={{0,2},{1,3},{2,0},{3,1},{4,6},{5,7},{6,4},{7,5},{8,10},{9,11},{10,... | collective-permute-start | bytes 589832 | tf_op jit(solution)/shard_map/ppermute | solution.py:119
  59.2 28.9 %collective-permute-start.13 = (bf16[2,2,1,32,768]{4,3,2,1,0:T(8,128)(2,1)S(1)}, bf16[2,2,1,32,768]{4,3,2,1,0:T(8,128)(2,1)S(1)}, u32[]{:S(2)}, u32[]{:S(2)}) collective-permute-start(bf16[2,2,1,32,768]{4,3,2,1,0:T(8,128)(2,1)S(1)} %reverse_select_fusion.2), channel_id=1, source_target_pairs={{0,3},{1,2},{2,1},{3,0},{4,7},{5,6},{6,5},{7,4},{8,11},{9,10},{10,... | collective-permute-start | bytes 589832 | tf_op jit(solution)/shard_map/ppermute | solution.py:119
  59.8 11.0 %collective-permute-start.4 = (bf16[64,3072]{1,0:T(8,128)(2,1)S(1)}, bf16[64,3072]{1,0:T(8,128)(2,1)S(1)}, u32[]{:S(2)}, u32[]{:S(2)}) collective-permute-start(bf16[64,3072]{1,0:T(8,128)(2,1)S(1)} %slice.129), channel_id=1, source_target_pairs={{0,16},{4,12},{8,24},{12,4},{16,0},{20,28},{24,8},{28,20},{1,17},{... | collective-permute-start | bytes 1179656 | tf_op jit(solution)/shard_map/ppermute | solution.py:43
  62.3 17.0 %collective-permute-start.9 = (bf16[128,3072]{1,0:T(8,128)(2,1)S(1)}, bf16[128,3072]{1,0:T(8,128)(2,1)S(1)}, u32[]{:S(2)}, u32[]{:S(2)}) collective-permute-start(bf16[128,3072]{1,0:T(8,128)(2,1)S(1)} %slice.132), channel_id=1, source_target_pairs={{0,8},{4,20},{8,0},{12,28},{16,24},{20,4},{24,16},{28,12},{1,9},{5... | collective-permute-start | bytes 2359304 | tf_op jit(solution)/shard_map/ppermute | solution.py:43
  64.1 15.2 %collective-permute-start.10 = (bf16[64,3072]{1,0:T(8,128)(2,1)S(1)}, bf16[64,3072]{1,0:T(8,128)(2,1)S(1)}, u32[]{:S(2)}, u32[]{:S(2)}) collective-permute-start(bf16[64,3072]{1,0:T(8,128)(2,1)S(1)} %slice.134), channel_id=1, source_target_pairs={{0,16},{4,12},{8,24},{12,4},{16,0},{20,28},{24,8},{28,20},{1,17},{... | collective-permute-start | bytes 1179656 | tf_op jit(solution)/shard_map/ppermute | solution.py:43
  91.2 16.4 %collective-permute-start.16 = (bf16[256,3072]{1,0:T(8,128)(2,1)S(1)}, bf16[256,3072]{1,0:T(8,128)(2,1)S(1)}, u32[]{:S(2)}, u32[]{:S(2)}) collective-permute-start(bf16[256,3072]{1,0:T(8,128)(2,1)S(1)} %get-tuple-element.99), channel_id=1, source_target_pairs={{0,4},{4,0},{8,12},{12,8},{16,20},{20,16},{24,28},{28,24},{1,5},{5... | collective-permute-start | bytes 4718600 | tf_op jit(solution)/shard_map/ppermute | solution.py:40
  91.8 12.1 %collective-permute-start.12 = (bf16[1,1,4,32,3072]{4,3,2,1,0:T(8,128)(2,1)S(1)}, bf16[1,1,4,32,3072]{4,3,2,1,0:T(8,128)(2,1)S(1)}, u32[]{:S(2)}, u32[]{:S(2)}) collective-permute-start(bf16[1,1,4,32,3072]{4,3,2,1,0:T(8,128)(2,1)S(1)} %get-tuple-element.78), channel_id=1, source_target_pairs={{0,16},{4,12},{8,24},{12,4},{16,0},{20,28},{24,8},{28,20},{1,17},{... | collective-permute-start | bytes 2359304 | tf_op jit(solution)/shard_map/ppermute | solution.py:43
  105.1 12.7 %collective-permute-start.15 = (bf16[1,2,4,32,1536]{4,3,2,1,0:T(8,128)(2,1)}, bf16[1,2,4,32,1536]{4,3,2,1,0:T(8,128)(2,1)}, u32[]{:S(2)}, u32[]{:S(2)}) collective-permute-start(bf16[1,2,4,32,1536]{4,3,2,1,0:T(8,128)(2,1)} %get-tuple-element.79), channel_id=1, source_target_pairs={{0,8},{4,20},{8,0},{12,28},{16,24},{20,4},{24,16},{28,12},{1,9},{5... | collective-permute-start | bytes 2359304 | tf_op jit(solution)/shard_map/ppermute | solution.py:43
  109.3 17.0 %collective-permute-start.18 = (bf16[128,3072]{1,0:T(8,128)(2,1)}, bf16[128,3072]{1,0:T(8,128)(2,1)}, u32[]{:S(2)}, u32[]{:S(2)}) collective-permute-start(bf16[128,3072]{1,0:T(8,128)(2,1)} %slice.139), channel_id=1, source_target_pairs={{0,8},{4,20},{8,0},{12,28},{16,24},{20,4},{24,16},{28,12},{1,9},{5... | collective-permute-start | bytes 2359304 | tf_op jit(solution)/shard_map/ppermute | solution.py:43
  109.3 29.5 %collective-permute-start.17 = (bf16[1,2,4,32,1536]{4,3,2,1,0:T(8,128)(2,1)}, bf16[1,2,4,32,1536]{4,3,2,1,0:T(8,128)(2,1)S(1)}, u32[]{:S(2)}, u32[]{:S(2)}) collective-permute-start(bf16[1,2,4,32,1536]{4,3,2,1,0:T(8,128)(2,1)} %get-tuple-element.80), channel_id=1, source_target_pairs={{0,8},{4,20},{8,0},{12,28},{16,24},{20,4},{24,16},{28,12},{1,9},{5... | collective-permute-start | bytes 2359304 | tf_op jit(solution)/shard_map/ppermute | solution.py:43
  127.7 11.2 %collective-permute-start.20 = (bf16[64,3072]{1,0:T(8,128)(2,1)S(1)}, bf16[64,3072]{1,0:T(8,128)(2,1)S(1)}, u32[]{:S(2)}, u32[]{:S(2)}) collective-permute-start(bf16[64,3072]{1,0:T(8,128)(2,1)S(1)} %slice.141), channel_id=1, source_target_pairs={{0,16},{4,12},{8,24},{12,4},{16,0},{20,28},{24,8},{28,20},{1,17},{... | collective-permute-start | bytes 1179656 | tf_op jit(solution)/shard_map/ppermute | solution.py:43
  130.8 16.8 %collective-permute-start.19 = (bf16[2,2,4,32,1536]{4,3,2,1,0:T(8,128)(2,1)S(1)}, bf16[2,2,4,32,1536]{4,3,2,1,0:T(8,128)(2,1)S(1)}, u32[]{:S(2)}, u32[]{:S(2)}) collective-permute-start(bf16[2,2,4,32,1536]{4,3,2,1,0:T(8,128)(2,1)S(1)} %pad_maximum_fusion.1), channel_id=1, source_target_pairs={{0,4},{4,0},{8,12},{12,8},{16,20},{20,16},{24,28},{28,24},{1,5},{5... | collective-permute-start | bytes 4718600 | tf_op jit(solution)/shard_map/ppermute | solution.py:40
  139.7 12.1 %collective-permute-start.22 = (bf16[1,1,4,32,3072]{4,3,2,1,0:T(8,128)(2,1)S(1)}, bf16[1,1,4,32,3072]{4,3,2,1,0:T(8,128)(2,1)S(1)}, u32[]{:S(2)}, u32[]{:S(2)}) collective-permute-start(bf16[1,1,4,32,3072]{4,3,2,1,0:T(8,128)(2,1)S(1)} %fusion.61), channel_id=1, source_target_pairs={{0,16},{4,12},{8,24},{12,4},{16,0},{20,28},{24,8},{28,20},{1,17},{... | collective-permute-start | bytes 2359304 | tf_op jit(solution)/shard_map/ppermute | solution.py:43
  141.4 16.7 %collective-permute-start.21 = (bf16[2,2,4,32,1536]{4,3,2,1,0:T(8,128)(2,1)S(1)}, bf16[2,2,4,32,1536]{4,3,2,1,0:T(8,128)(2,1)}, u32[]{:S(2)}, u32[]{:S(2)}) collective-permute-start(bf16[2,2,4,32,1536]{4,3,2,1,0:T(8,128)(2,1)S(1)} %pad_maximum_fusion.2), channel_id=1, source_target_pairs={{0,4},{4,0},{8,12},{12,8},{16,20},{20,16},{24,28},{28,24},{1,5},{5... | collective-permute-start | bytes 4718600 | tf_op jit(solution)/shard_map/ppermute | solution.py:40
  151.9 17.5 %collective-permute-start.24 = (bf16[1,2,4,32,1536]{4,3,2,1,0:T(8,128)(2,1)S(1)}, bf16[1,2,4,32,1536]{4,3,2,1,0:T(8,128)(2,1)}, u32[]{:S(2)}, u32[]{:S(2)}) collective-permute-start(bf16[1,2,4,32,1536]{4,3,2,1,0:T(8,128)(2,1)S(1)} %get-tuple-element.76), channel_id=1, source_target_pairs={{0,8},{4,20},{8,0},{12,28},{16,24},{20,4},{24,16},{28,12},{1,9},{5... | collective-permute-start | bytes 2359304 | tf_op jit(solution)/shard_map/ppermute | solution.py:43
  154.0 21.4 %collective-permute-start.26 = (bf16[1,2,4,32,1536]{4,3,2,1,0:T(8,128)(2,1)S(1)}, bf16[1,2,4,32,1536]{4,3,2,1,0:T(8,128)(2,1)}, u32[]{:S(2)}, u32[]{:S(2)}) collective-permute-start(bf16[1,2,4,32,1536]{4,3,2,1,0:T(8,128)(2,1)S(1)} %get-tuple-element.75), channel_id=1, source_target_pairs={{0,8},{4,20},{8,0},{12,28},{16,24},{20,4},{24,16},{28,12},{1,9},{5... | collective-permute-start | bytes 2359304 | tf_op jit(solution)/shard_map/ppermute | solution.py:43
  164.2 8.7 %collective-permute-start.23 = (bf16[2,2,2,32,768]{4,3,1,0,2:T(8,128)(2,1)S(1)}, bf16[2,2,2,32,768]{4,3,1,0,2:T(8,128)(2,1)S(1)}, u32[]{:S(2)}, u32[]{:S(2)}) collective-permute-start(bf16[2,2,2,32,768]{4,3,1,0,2:T(8,128)(2,1)S(1)} %bitcast.132), channel_id=1, source_target_pairs={{0,1},{1,0},{2,3},{3,2},{4,5},{5,4},{6,7},{7,6},{8,9},{9,8},{10,11... | collective-permute-start | bytes 1179656 | tf_op jit(solution)/shard_map/ppermute | solution.py:119
  175.4 10.6 %collective-permute-start.28 = (bf16[2,2,4,32,1536]{4,3,2,1,0:T(8,128)(2,1)}, bf16[2,2,4,32,1536]{4,3,2,1,0:T(8,128)(2,1)}, u32[]{:S(2)}, u32[]{:S(2)}) collective-permute-start(bf16[2,2,4,32,1536]{4,3,2,1,0:T(8,128)(2,1)} %pad_maximum_fusion.5), channel_id=1, source_target_pairs={{0,4},{4,0},{8,12},{12,8},{16,20},{20,16},{24,28},{28,24},{1,5},{5... | collective-permute-start | bytes 4718600 | tf_op jit(solution)/shard_map/ppermute | solution.py:40
  179.1 15.5 %collective-permute-start.25 = (bf16[2,2,1,32,768]{4,3,2,1,0:T(8,128)(2,1)}, bf16[2,2,1,32,768]{4,3,2,1,0:T(8,128)(2,1)}, u32[]{:S(2)}, u32[]{:S(2)}) collective-permute-start(bf16[2,2,1,32,768]{4,3,2,1,0:T(8,128)(2,1)} %slice_bitcast_fusion), channel_id=1, source_target_pairs={{0,2},{1,3},{2,0},{3,1},{4,6},{5,7},{6,4},{7,5},{8,10},{9,11},{10,... | collective-permute-start | bytes 589832 | tf_op jit(solution)/shard_map/ppermute | solution.py:119
  (24 other events, 134.5 us)
